TPU v7x, 1024 devices: a whole 4x4x32 slice. The times are simulated.
1024 devices in a mesh: dp: 128 (over z_lo, x, core), group: 8 (over z_hi, y).
Axes of the slice: x: 4, y: 4, z: 32 (z_hi: 2, z_lo: 16; z = z_hi * 16 + z_lo), core: 2. Of those that a mesh axis runs over, the one named last changes fastest.
Arguments:
- images: bfloat16 [393216, 1152], P(('dp', 'group')), may hold values from -6 to 6
- texts: bfloat16 [393216, 1152], P(('dp', 'group')), may hold values from -6 to 6
- logit_scale: float32 [1], replicated, may hold values from 40 to 120
- logit_bias: float32 [1], replicated, may hold values from -3 to 3
Outputs:
- row_loss: float32 [393216], P(('dp', 'group'))
- image_grad: bfloat16 [393216, 1152], P(('dp', 'group'))
- text_grad: bfloat16 [393216, 1152], P(('dp', 'group'))
All inputs are finite; a program needn't handle non-finite values.
Results may differ from a plain program's by a relative error of at most 0.0075.
Values may be sent and summed in bfloat16 or wider, within the bound.
No kernel may reach another device: no remote copies, remote signals or barrier semaphores. Data moves between devices by JAX's collectives and lax.ppermute only.
A program may use at most 32 MiB of HBM per device.

v0:
```python
import jax
import jax.numpy as jnp
from jax import lax
from jax.sharding import PartitionSpec as P


def from_behind(value, axis, steps):
    count = lax.axis_size(axis)
    pairs = [(source, (source + steps) % count) for source in range(count)]
    return lax.ppermute(value, axis, pairs)


def normalize(embedded):
    values = embedded.astype(jnp.float32)
    factor = lax.rsqrt(jnp.sum(values * values, axis=1, keepdims=True) + 1e-06)
    return (values * factor, factor)


def unit_backward(unit_grad, unit, factor):
    inner = jnp.sum(unit_grad * unit, axis=1, keepdims=True)
    return (factor * (unit_grad - unit * inner)).astype(jnp.bfloat16)


def pair_block(image_low, text_low, labels, scale_value, bias_value):
    logits = (
        scale_value
        * jnp.einsum("id,jd->ij", image_low, text_low, preferred_element_type=jnp.float32)
        + bias_value
    )
    signed = labels * logits
    losses = jnp.sum(jax.nn.softplus(-signed), axis=1)
    pair_weights = (-scale_value * labels * jax.nn.sigmoid(-signed)).astype(jnp.bfloat16)
    image_part = jnp.einsum("ij,jd->id", pair_weights, text_low, preferred_element_type=jnp.float32)
    text_part = jnp.einsum("ij,id->jd", pair_weights, image_low, preferred_element_type=jnp.float32)
    return (losses, image_part, text_part)


def shards(images, texts, logit_scale, logit_bias):
    count_rows = images.shape[0]
    scale_value = logit_scale[0]
    bias_value = logit_bias[0]
    diagonal = 2.0 * jnp.eye(count_rows, dtype=jnp.float32) - 1.0
    others = -jnp.ones((count_rows, count_rows), jnp.float32)
    image_unit, image_factor = normalize(images)
    image_low = image_unit.astype(jnp.bfloat16)
    text_unit, text_factor = normalize(texts)
    text_low = text_unit.astype(jnp.bfloat16)
    loss_own, image_own, text_own = pair_block(
        image_low, text_low, diagonal, scale_value, bias_value
    )
    text_one = from_behind(text_low, ("dp", "group"), 1)
    loss_first, image_first, text_first = pair_block(
        image_low, text_one, others, scale_value, bias_value
    )
    term_one = text_first.astype(jnp.bfloat16)
    text_two, moved_term = from_behind((text_one, term_one), ("dp", "group"), 1)
    loss_second, image_second, text_second = pair_block(
        image_low, text_two, others, scale_value, bias_value
    )
    term_two = text_second.astype(jnp.bfloat16)
    back_first, back_second = from_behind((moved_term, term_two), ("dp", "group"), -2)
    row_loss = (loss_own + loss_first + loss_second) / (3.0 * count_rows)
    image_total = image_own + image_first + image_second
    text_total = text_own + back_first.astype(jnp.float32) + back_second.astype(jnp.float32)
    image_grad = unit_backward(image_total, image_unit, image_factor)
    text_grad = unit_backward(text_total, text_unit, text_factor)
    return (row_loss, image_grad, text_grad)


def solution(mesh):
    placed = (P(("dp", "group"), None), P(("dp", "group"), None), P(), P())
    return jax.shard_map(
        shards,
        mesh=mesh,
        in_specs=placed,
        out_specs=(P(("dp", "group")), P(("dp", "group"), None), P(("dp", "group"), None)),
        check_vma=False,
    )
```

profile of v0, /device:TPU:414, one launch (start us, length us, event | category | flops | bytes accessed | tf_op | source)
XLA Modules:
  0.0 744.3 jit_solution(14407588793910847533)
XLA Ops:
  0.6 0.0 copy-start.1
  0.6 1.5 fusion.15
  2.1 1.4 fusion.2
  3.5 14.2 %collective-permute-start = (bf16[384,1152]{1,0:T(8,128)(2,1)S(1)}, bf16[384,1152]{1,0:T(8,128)(2,1)S(1)}, u32[]{:S(2)}, u32[]{:S(2)}) collective-permute-start(bf16[384,1152]{1,0:T(8,128)(2,1)S(1)} %fusion.2), channel_id=1, source_target_pairs={{0,1},{1,2},{2,3},{3,4},{4,5},{5,6},{6,7},{7,8},{8,9},{9,10},{10,1... | collective-permute-start | bytes 2654216 | tf_op jit(solution)/shard_map/ppermute | solution.py:10
  17.8 0.0 copy-done.1
  17.8 0.3 fusion.10
  19.3 1.1 fusion.22
  20.4 0.7 fusion.26
  21.2 140.5 %collective-permute-done = bf16[384,1152]{1,0:T(8,128)(2,1)S(1)} collective-permute-done((bf16[384,1152]{1,0:T(8,128)(2,1)S(1)}, bf16[384,1152]{1,0:T(8,128)(2,1)S(1)}, u32[]{:S(2)}, u32[]{:S(2)}) %collective-permute-start) | collective-permute-done | bytes 884768 | tf_op jit(solution)/shard_map/ppermute | solution.py:10
  161.7 25.6 %collective-permute-start.1 = (bf16[384,1152]{1,0:T(8,128)(2,1)S(1)}, bf16[384,1152]{1,0:T(8,128)(2,1)S(1)}, u32[]{:S(2)}, u32[]{:S(2)}) collective-permute-start(bf16[384,1152]{1,0:T(8,128)(2,1)S(1)} %collective-permute-done), channel_id=1, source_target_pairs={{0,1},{1,2},{2,3},{3,4},{4,5},{5,6},{6,7},{7,8},{8,9},{9,10},{10,1... | collective-permute-start | bytes 2654216 | tf_op jit(solution)/shard_map/ppermute | solution.py:10
  187.3 1.1 fusion.23
  188.4 0.7 convolution_convert_fusion.1
  189.2 1.9 collective-permute-start.2
  191.1 0.7 convolution_add_fusion.1
  191.8 273.6 %collective-permute-done.1 = bf16[384,1152]{1,0:T(8,128)(2,1)S(1)} collective-permute-done((bf16[384,1152]{1,0:T(8,128)(2,1)S(1)}, bf16[384,1152]{1,0:T(8,128)(2,1)S(1)}, u32[]{:S(2)}, u32[]{:S(2)}) %collective-permute-start.1) | collective-permute-done | bytes 884768 | tf_op jit(solution)/shard_map/ppermute | solution.py:10
  465.4 1.1 fusion.24
  466.5 0.7 convolution_convert_fusion
  467.2 1.9 collective-permute-start.4
  469.2 19.1 %collective-permute-done.2 = bf16[384,1152]{1,0:T(8,128)(2,1)S(1)} collective-permute-done((bf16[384,1152]{1,0:T(8,128)(2,1)S(1)}, bf16[384,1152]{1,0:T(8,128)(2,1)S(1)}, u32[]{:S(2)}, u32[]{:S(2)}) %collective-permute-start.2) | collective-permute-done | bytes 884768 | tf_op jit(solution)/shard_map/ppermute | solution.py:10
  488.3 1.9 collective-permute-start.3
  490.2 1.0 fusion.6
  491.2 0.6 add_multiply_fusion
  491.8 0.0 copy-start
  491.8 1.3 fusion.9
  493.1 24.7 %collective-permute-done.4 = bf16[384,1152]{1,0:T(8,128)(2,1)S(1)} collective-permute-done((bf16[384,1152]{1,0:T(8,128)(2,1)S(1)}, bf16[384,1152]{1,0:T(8,128)(2,1)S(1)}, u32[]{:S(2)}, u32[]{:S(2)}) %collective-permute-start.4) | collective-permute-done | bytes 884768 | tf_op jit(solution)/shard_map/ppermute | solution.py:10
  517.8 224.0 %collective-permute-done.3 = bf16[384,1152]{1,0:T(8,128)(2,1)S(1)} collective-permute-done((bf16[384,1152]{1,0:T(8,128)(2,1)S(1)}, bf16[384,1152]{1,0:T(8,128)(2,1)S(1)}, u32[]{:S(2)}, u32[]{:S(2)}) %collective-permute-start.3) | collective-permute-done | bytes 884768 | tf_op jit(solution)/shard_map/ppermute | solution.py:10
  741.8 0.0 copy-done
  741.8 1.0 fusion.11
  742.8 1.5 fusion.14
  (2 shorter events, 0.0 us)
Async XLA Ops:
  0.6 17.1 %copy-start.1 = (bf16[384,1152]{1,0:T(8,128)(2,1)S(1)}, bf16[384,1152]{1,0:T(8,128)(2,1)}, u32[]{:S(2)}) copy-start(bf16[384,1152]{1,0:T(8,128)(2,1)} %param.4) | copy-start | bytes 2654212
  3.5 158.2 %collective-permute-start = (bf16[384,1152]{1,0:T(8,128)(2,1)S(1)}, bf16[384,1152]{1,0:T(8,128)(2,1)S(1)}, u32[]{:S(2)}, u32[]{:S(2)}) collective-permute-start(bf16[384,1152]{1,0:T(8,128)(2,1)S(1)} %fusion.2), channel_id=1, source_target_pairs={{0,1},{1,2},{2,3},{3,4},{4,5},{5,6},{6,7},{7,8},{8,9},{9,10},{10,1... | collective-permute-start | bytes 2654216 | tf_op jit(solution)/shard_map/ppermute | solution.py:10
  161.7 303.7 %collective-permute-start.1 = (bf16[384,1152]{1,0:T(8,128)(2,1)S(1)}, bf16[384,1152]{1,0:T(8,128)(2,1)S(1)}, u32[]{:S(2)}, u32[]{:S(2)}) collective-permute-start(bf16[384,1152]{1,0:T(8,128)(2,1)S(1)} %collective-permute-done), channel_id=1, source_target_pairs={{0,1},{1,2},{2,3},{3,4},{4,5},{5,6},{6,7},{7,8},{8,9},{9,10},{10,1... | collective-permute-start | bytes 2654216 | tf_op jit(solution)/shard_map/ppermute | solution.py:10
  189.2 299.1 %collective-permute-start.2 = (bf16[384,1152]{1,0:T(8,128)(2,1)S(1)}, bf16[384,1152]{1,0:T(8,128)(2,1)S(1)}, u32[]{:S(2)}, u32[]{:S(2)}) collective-permute-start(bf16[384,1152]{1,0:T(8,128)(2,1)S(1)} %convolution_convert_fusion.1), channel_id=1, source_target_pairs={{0,1},{1,2},{2,3},{3,4},{4,5},{5,6},{6,7},{7,8},{8,9},{9,10},{10,1... | collective-permute-start | bytes 2654216 | tf_op jit(solution)/shard_map/ppermute | solution.py:10
  467.2 50.5 %collective-permute-start.4 = (bf16[384,1152]{1,0:T(8,128)(2,1)S(1)}, bf16[384,1152]{1,0:T(8,128)(2,1)S(1)}, u32[]{:S(2)}, u32[]{:S(2)}) collective-permute-start(bf16[384,1152]{1,0:T(8,128)(2,1)S(1)} %convolution_convert_fusion), channel_id=1, source_target_pairs={{0,1022},{1,1023},{2,0},{3,1},{4,2},{5,3},{6,4},{7,5},{8,6},{9,7},... | collective-permute-start | bytes 2654216 | tf_op jit(solution)/shard_map/ppermute | solution.py:10
  488.3 253.5 %collective-permute-start.3 = (bf16[384,1152]{1,0:T(8,128)(2,1)S(1)}, bf16[384,1152]{1,0:T(8,128)(2,1)S(1)}, u32[]{:S(2)}, u32[]{:S(2)}) collective-permute-start(bf16[384,1152]{1,0:T(8,128)(2,1)S(1)} %collective-permute-done.2), channel_id=1, source_target_pairs={{0,1022},{1,1023},{2,0},{3,1},{4,2},{5,3},{6,4},{7,5},{8,6},{9,7},... | collective-permute-start | bytes 2654216 | tf_op jit(solution)/shard_map/ppermute | solution.py:10
  491.8 250.0 %copy-start = (bf16[384,1152]{1,0:T(8,128)(2,1)S(1)}, bf16[384,1152]{1,0:T(8,128)(2,1)}, u32[]{:S(2)}) copy-start(bf16[384,1152]{1,0:T(8,128)(2,1)} %param.5) | copy-start | bytes 2654212
where the time goes:
time: 745 us; the launch traced here: 744 us
  waiting for transfers between devices  682 us (92%)
  starting transfers between devices  45.6 us (6%)
  matrix products  8.17 us (1%)
    ppermute x5, waiting for transfers between devices, from_behind(): return lax.ppermute(value, axis, pairs)  682 us
    ppermute x5, starting transfers between devices, from_behind(): return lax.ppermute(value, axis, pairs)  45.6 us
  transfers between devices with their start and end apart: 5, of which 5 were waited for; matrix products, arithmetic and copies ran while one was open for 1% of the time, Pallas kernels for 0%

commit v1 on v0

v1 whole, which is shorter than its diff:
```python
import jax
import jax.numpy as jnp
from jax import lax
from jax.sharding import PartitionSpec as P

AXES = ("dp", "group")
RUN = 4
CHUNKS = 1


def within(value, hops):
    count = lax.axis_size(AXES)
    pairs = [
        (base + a, base + b) for base in range(0, count, RUN) for a, b in sorted(hops.items())
    ]
    return lax.ppermute(value, AXES, pairs)


def across(value):
    count = lax.axis_size(AXES)
    pairs = [(p, (p + (2 if p % RUN >= 2 else -2)) % count) for p in range(count)]
    return lax.ppermute(value, AXES, pairs)


def normalize(embedded):
    values = embedded.astype(jnp.float32)
    factor = lax.rsqrt(jnp.sum(values * values, axis=1, keepdims=True) + 1e-06)
    return (values * factor, factor)


def low(embedded):
    return normalize(embedded)[0].astype(jnp.bfloat16)


def unit_backward(unit_grad, unit, factor):
    inner = jnp.sum(unit_grad * unit, axis=1, keepdims=True)
    return (factor * (unit_grad - unit * inner)).astype(jnp.bfloat16)


def logits_of(rows, columns, scale_value, bias_value):
    dots = jnp.einsum("id,jd->ij", rows, columns, preferred_element_type=jnp.float32)
    return scale_value * dots + bias_value


def apply(weights, values):
    return jnp.einsum("ij,jd->id", weights, values, preferred_element_type=jnp.float32)


def negative_pairs(rows, columns, scale_value, bias_value):
    logits = logits_of(rows, columns, scale_value, bias_value)
    losses = jnp.sum(jax.nn.softplus(logits), axis=1)
    weights = (scale_value * jax.nn.sigmoid(logits)).astype(jnp.bfloat16)
    return losses, apply(weights, columns)


def shards(images, texts, logit_scale, logit_bias):
    count_rows = images.shape[0]
    scale_value, bias_value = logit_scale[0], logit_bias[0]
    place = lax.axis_index(AXES) % RUN
    first_half = place < 2
    inner = (place == 1) | (place == 2)
    raw_a = jnp.where(first_half, images, texts)
    raw_b = jnp.where(first_half, texts, images)
    step = count_rows // CHUNKS
    far = [across(raw_a[i * step : (i + 1) * step]) for i in range(CHUNKS)]
    near_two = within(raw_b, {0: 2, 2: 0, 1: 3, 3: 1})
    near_one = within(jnp.where(inner, raw_a, raw_b), {1: 0, 2: 3, 0: 1, 3: 2})
    near_mid = within(raw_b, {2: 1, 1: 2})

    unit_a, factor_a = normalize(raw_a)
    unit_b, factor_b = normalize(raw_b)
    low_a, low_b = unit_a.astype(jnp.bfloat16), unit_b.astype(jnp.bfloat16)

    labels = 2.0 * jnp.eye(count_rows, dtype=jnp.float32) - 1.0
    signed = labels * logits_of(low_a, low_b, scale_value, bias_value)
    plus = jax.nn.softplus(-signed)
    own_loss = jnp.where(first_half, jnp.sum(plus, axis=1), jnp.sum(plus, axis=0))
    weights = (-scale_value * labels * jax.nn.sigmoid(-signed)).astype(jnp.bfloat16)
    grad_a = apply(weights, low_b)
    grad_b = jnp.einsum("ij,id->jd", weights, low_a, preferred_element_type=jnp.float32)

    loss_two, part = negative_pairs(low_b, low(near_two), scale_value, bias_value)
    grad_b = grad_b + part
    early = jnp.where(inner, near_mid, near_one)
    loss_one, part = negative_pairs(low_b, low(early), scale_value, bias_value)
    grad_b = grad_b + part
    out_b = unit_backward(grad_b, unit_b, factor_b)
    loss_b = loss_two + loss_one

    loss_a = jnp.zeros_like(loss_b)
    relayed = [within(piece, {1: 0, 2: 3}) for piece in far]
    for piece in far:
        loss, part = negative_pairs(low_a, low(piece), scale_value, bias_value)
        grad_a, loss_a = grad_a + part, loss_a + loss
    for i, piece in enumerate(relayed):
        late = jnp.where(inner, near_one[i * step : (i + 1) * step], piece)
        loss, part = negative_pairs(low_a, low(late), scale_value, bias_value)
        grad_a, loss_a = grad_a + part, loss_a + loss
    out_a = unit_backward(grad_a, unit_a, factor_a)

    row_loss = (own_loss + jnp.where(first_half, loss_a, loss_b)) / (3.0 * count_rows)
    return (row_loss, jnp.where(first_half, out_a, out_b), jnp.where(first_half, out_b, out_a))


def solution(mesh):
    placed = (P(AXES, None), P(AXES, None), P(), P())
    return jax.shard_map(
        shards,
        mesh=mesh,
        in_specs=placed,
        out_specs=(P(AXES), P(AXES, None), P(AXES, None)),
        check_vma=False,
    )
```

time: 745 us -> 280 us (0.38)
  the two profiles are of different devices: /device:TPU:414 before, /device:TPU:32 now
where the time goes in v1:
time: 280 us
  waiting for transfers between devices  213 us (76%)
  starting transfers between devices  41.8 us (15%)
  matrix products  12.9 us (5%)
  other arithmetic  10 us (4%)
    ppermute x1, waiting for transfers between devices, across(): return lax.ppermute(value, AXES, pairs)  205 us
    ppermute x1, starting transfers between devices, across(): return lax.ppermute(value, AXES, pairs)  31.9 us
    ppermute x4, starting transfers between devices, within(): return lax.ppermute(value, AXES, pairs)  9.94 us
    ppermute x4, waiting for transfers between devices, within(): return lax.ppermute(value, AXES, pairs)  7.56 us
    dot_general x5, matrix products, logits_of(): jnp.einsum('id,jd->ij', rows, columns, preferred_element_type=jnp.float32)  6.79 us
    reduce_sum x5, other arithmetic, normalize(): factor = lax.rsqrt(jnp.sum(values * values, axis=1, keepdims=True) + 1e-06)  5.62 us
  transfers between devices with their start and end apart: 5, of which 2 were waited for; matrix products, arithmetic and copies ran while one was open for 4% of the time, Pallas kernels for 0%

profile of v1, /device:TPU:32, one launch (start us, length us, event | category | flops | bytes accessed | tf_op | source)
XLA Modules:
  0.0 279.9 jit_solution(1863824360718749293)
XLA Ops:
  0.6 0.0 copy-start
  0.6 0.0 copy-start.1
  0.7 1.7 fusion.10
  2.4 31.9 %collective-permute-start = (bf16[384,1152]{1,0:T(8,128)(2,1)S(1)}, bf16[384,1152]{1,0:T(8,128)(2,1)}, u32[]{:S(2)}, u32[]{:S(2)}) collective-permute-start(bf16[384,1152]{1,0:T(8,128)(2,1)S(1)} %get-tuple-element.11), channel_id=1, source_target_pairs={{0,1022},{1,1023},{2,4},{3,5},{4,2},{5,3},{6,8},{7,9},{8,6},{9,7},... | collective-permute-start | bytes 2654216 | tf_op jit(solution)/shard_map/ppermute | solution.py:22
  34.3 0.0 copy-done
  34.3 0.0 copy-done.1
  34.3 1.1 broadcast_select_fusion.2
  35.4 0.7 collective-permute-start.4
  36.1 5.8 %collective-permute-start.3 = (bf16[384,1152]{1,0:T(8,128)(2,1)S(1)}, bf16[384,1152]{1,0:T(8,128)(2,1)S(1)}, u32[]{:S(2)}, u32[]{:S(2)}) collective-permute-start(bf16[384,1152]{1,0:T(8,128)(2,1)S(1)} %get-tuple-element.15), channel_id=1, source_target_pairs={{0,2},{1,3},{2,0},{3,1},{4,6},{5,7},{6,4},{7,5},{8,10},{9,11},{10,... | collective-permute-start | bytes 2654216 | tf_op jit(solution)/shard_map/ppermute | solution.py:16
  41.9 1.9 collective-permute-start.1
  43.8 0.3 fusion.15
  45.4 1.2 fusion.50
  46.6 0.7 fusion.57
  47.3 0.8 fusion.56
  48.2 205.4 %collective-permute-done = bf16[384,1152]{1,0:T(8,128)(2,1)} collective-permute-done((bf16[384,1152]{1,0:T(8,128)(2,1)S(1)}, bf16[384,1152]{1,0:T(8,128)(2,1)}, u32[]{:S(2)}, u32[]{:S(2)}) %collective-permute-start) | collective-permute-done | bytes 884768 | tf_op jit(solution)/shard_map/ppermute | solution.py:22
  253.6 1.4 fusion.16
  255.1 0.0 collective-permute-done.3
  255.1 0.3 fusion.20
  255.3 1.5 collective-permute-start.2
  256.8 2.3 fusion.30
  259.1 1.1 fusion.32
  260.2 1.9 convolution_add_fusion.3
  262.1 0.8 convolution_add_fusion.1
  262.9 0.0 collective-permute-done.1
  262.9 0.0 collective-permute-done.4
  262.9 7.6 %collective-permute-done.2 = bf16[384,1152]{1,0:T(8,128)(2,1)S(1)} collective-permute-done((bf16[384,1152]{1,0:T(8,128)(2,1)}, bf16[384,1152]{1,0:T(8,128)(2,1)S(1)}, u32[]{:S(2)}, u32[]{:S(2)}) %collective-permute-start.2) | collective-permute-done | bytes 884768 | tf_op jit(solution)/shard_map/ppermute | solution.py:16
  270.5 2.0 fusion.18
  272.5 1.1 fusion.31
  273.6 0.9 fusion.6
  274.5 1.1 fusion.33
  275.7 0.9 fusion.11
  276.6 1.7 broadcast_select_fusion.3
  278.3 1.0 broadcast_select_fusion.4
  279.3 0.6 add_multiply_fusion
  (5 shorter events, 0.0 us)
Async XLA Ops:
  0.6 33.6 %copy-start = (bf16[384,1152]{1,0:T(8,128)(2,1)S(1)}, bf16[384,1152]{1,0:T(8,128)(2,1)}, u32[]{:S(2)}) copy-start(bf16[384,1152]{1,0:T(8,128)(2,1)} %param.4) | copy-start | bytes 2654212
  0.6 33.6 %copy-start.1 = (bf16[384,1152]{1,0:T(8,128)(2,1)S(1)}, bf16[384,1152]{1,0:T(8,128)(2,1)}, u32[]{:S(2)}) copy-start(bf16[384,1152]{1,0:T(8,128)(2,1)} %param.5) | copy-start | bytes 2654212
  2.4 251.3 %collective-permute-start = (bf16[384,1152]{1,0:T(8,128)(2,1)S(1)}, bf16[384,1152]{1,0:T(8,128)(2,1)}, u32[]{:S(2)}, u32[]{:S(2)}) collective-permute-start(bf16[384,1152]{1,0:T(8,128)(2,1)S(1)} %get-tuple-element.11), channel_id=1, source_target_pairs={{0,1022},{1,1023},{2,4},{3,5},{4,2},{5,3},{6,8},{7,9},{8,6},{9,7},... | collective-permute-start | bytes 2654216 | tf_op jit(solution)/shard_map/ppermute | solution.py:22
  35.4 227.6 %collective-permute-start.4 = (bf16[384,1152]{1,0:T(8,128)(2,1)S(1)}, bf16[384,1152]{1,0:T(8,128)(2,1)S(1)}, u32[]{:S(2)}, u32[]{:S(2)}) collective-permute-start(bf16[384,1152]{1,0:T(8,128)(2,1)S(1)} %get-tuple-element.15), channel_id=1, source_target_pairs={{1,2},{2,1},{5,6},{6,5},{9,10},{10,9},{13,14},{14,13},{17,18},{18,... | collective-permute-start | bytes 2654216 | tf_op jit(solution)/shard_map/ppermute | solution.py:16
  36.1 219.0 %collective-permute-start.3 = (bf16[384,1152]{1,0:T(8,128)(2,1)S(1)}, bf16[384,1152]{1,0:T(8,128)(2,1)S(1)}, u32[]{:S(2)}, u32[]{:S(2)}) collective-permute-start(bf16[384,1152]{1,0:T(8,128)(2,1)S(1)} %get-tuple-element.15), channel_id=1, source_target_pairs={{0,2},{1,3},{2,0},{3,1},{4,6},{5,7},{6,4},{7,5},{8,10},{9,11},{10,... | collective-permute-start | bytes 2654216 | tf_op jit(solution)/shard_map/ppermute | solution.py:16
  41.9 221.0 %collective-permute-start.1 = (bf16[384,1152]{1,0:T(8,128)(2,1)}, bf16[384,1152]{1,0:T(8,128)(2,1)}, u32[]{:S(2)}, u32[]{:S(2)}) collective-permute-start(bf16[384,1152]{1,0:T(8,128)(2,1)} %get-tuple-element.14), channel_id=1, source_target_pairs={{0,1},{1,0},{2,3},{3,2},{4,5},{5,4},{6,7},{7,6},{8,9},{9,8},{10,11... | collective-permute-start | bytes 2654216 | tf_op jit(solution)/shard_map/ppermute | solution.py:16
  255.3 15.1 %collective-permute-start.2 = (bf16[384,1152]{1,0:T(8,128)(2,1)}, bf16[384,1152]{1,0:T(8,128)(2,1)S(1)}, u32[]{:S(2)}, u32[]{:S(2)}) collective-permute-start(bf16[384,1152]{1,0:T(8,128)(2,1)} %collective-permute-done), channel_id=1, source_target_pairs={{1,0},{2,3},{5,4},{6,7},{9,8},{10,11},{13,12},{14,15},{17,16},{18,... | collective-permute-start | bytes 2654216 | tf_op jit(solution)/shard_map/ppermute | solution.py:16

commit v2 on v1

--- a/solution.py
+++ b/solution.py
@@ -5,7 +5,33 @@
 
 AXES = ("dp", "group")
 RUN = 4
-CHUNKS = 1
+LAYER = 16
+PARTS = ((0, 384),)
+
+
+def tables(count):
+    runs = count // RUN
+    far, shift, relay = [], [], []
+    middle = [(0, count - 1), (count - 1, 0)]
+    for run in range(runs):
+        middle += [(run * RUN + 1, run * RUN + 2), (run * RUN + 2, run * RUN + 1)]
+        step = run % LAYER == LAYER - 1
+        slot = (run + 1 - (LAYER if step else 0)) % runs
+        final = (run + 1) % runs
+        far += [(run * RUN + y, slot * RUN + y - 2) for y in (2, 3)]
+        if step:
+            shift += [(slot * RUN + y, final * RUN + y) for y in (0, 1)]
+        if final != 0:
+            relay += [(slot * RUN + 1, final * RUN)]
+        step = run % LAYER == 0
+        slot = (run - 1 + (LAYER if step else 0)) % runs
+        final = (run - 1) % runs
+        far += [(run * RUN + y, slot * RUN + y + 2) for y in (0, 1)]
+        if step:
+            shift += [(slot * RUN + y, final * RUN + y) for y in (2, 3)]
+        if run != 0:
+            relay += [(slot * RUN + 2, final * RUN + 3)]
+    return far, shift, relay, middle
 
 
 def within(value, hops):
@@ -13,12 +39,6 @@
     pairs = [
         (base + a, base + b) for base in range(0, count, RUN) for a, b in sorted(hops.items())
     ]
-    return lax.ppermute(value, AXES, pairs)
-
-
-def across(value):
-    count = lax.axis_size(AXES)
-    pairs = [(p, (p + (2 if p % RUN >= 2 else -2)) % count) for p in range(count)]
     return lax.ppermute(value, AXES, pairs)
 
 
@@ -56,20 +76,23 @@
 def shards(images, texts, logit_scale, logit_bias):
     count_rows = images.shape[0]
     scale_value, bias_value = logit_scale[0], logit_bias[0]
-    place = lax.axis_index(AXES) % RUN
+    index = lax.axis_index(AXES)
+    count = lax.axis_size(AXES)
+    place, run = index % RUN, index // RUN
     first_half = place < 2
     inner = (place == 1) | (place == 2)
+    shifted = jnp.where(first_half, run % LAYER == 0, run % LAYER == LAYER - 1)
+    end = (index == 0) | (index == count - 1)
+    far_pairs, shift_pairs, relay_pairs, middle_pairs = tables(count)
     raw_a = jnp.where(first_half, images, texts)
     raw_b = jnp.where(first_half, texts, images)
-    step = count_rows // CHUNKS
-    far = [across(raw_a[i * step : (i + 1) * step]) for i in range(CHUNKS)]
-    near_two = within(raw_b, {0: 2, 2: 0, 1: 3, 3: 1})
-    near_one = within(jnp.where(inner, raw_a, raw_b), {1: 0, 2: 3, 0: 1, 3: 2})
-    near_mid = within(raw_b, {2: 1, 1: 2})
-
+    far = [lax.ppermute(raw_a[a:b], AXES, far_pairs) for a, b in PARTS]
     unit_a, factor_a = normalize(raw_a)
     unit_b, factor_b = normalize(raw_b)
     low_a, low_b = unit_a.astype(jnp.bfloat16), unit_b.astype(jnp.bfloat16)
+    near_two = within(low_b, {0: 2, 2: 0, 1: 3, 3: 1})
+    near_one = within(jnp.where(inner, low_a, low_b), {1: 0, 2: 3, 0: 1, 3: 2})
+    middle = lax.ppermute(jnp.where(inner, low_b, low_a), AXES, middle_pairs)
 
     labels = 2.0 * jnp.eye(count_rows, dtype=jnp.float32) - 1.0
     signed = labels * logits_of(low_a, low_b, scale_value, bias_value)
@@ -79,22 +102,24 @@
     grad_a = apply(weights, low_b)
     grad_b = jnp.einsum("ij,id->jd", weights, low_a, preferred_element_type=jnp.float32)
 
-    loss_two, part = negative_pairs(low_b, low(near_two), scale_value, bias_value)
+    loss_two, part = negative_pairs(low_b, near_two, scale_value, bias_value)
     grad_b = grad_b + part
-    early = jnp.where(inner, near_mid, near_one)
-    loss_one, part = negative_pairs(low_b, low(early), scale_value, bias_value)
+    early = jnp.where(inner, middle, near_one)
+    loss_one, part = negative_pairs(low_b, early, scale_value, bias_value)
     grad_b = grad_b + part
     out_b = unit_backward(grad_b, unit_b, factor_b)
     loss_b = loss_two + loss_one
 
+    held = jnp.where(inner, near_one, middle)
     loss_a = jnp.zeros_like(loss_b)
-    relayed = [within(piece, {1: 0, 2: 3}) for piece in far]
-    for piece in far:
-        loss, part = negative_pairs(low_a, low(piece), scale_value, bias_value)
+    for (a, b), piece in zip(PARTS, far):
+        moved = lax.ppermute(piece, AXES, shift_pairs)
+        relayed = lax.ppermute(piece, AXES, relay_pairs)
+        two = low(jnp.where(shifted, moved, piece))
+        loss, part = negative_pairs(low_a, two, scale_value, bias_value)
         grad_a, loss_a = grad_a + part, loss_a + loss
-    for i, piece in enumerate(relayed):
-        late = jnp.where(inner, near_one[i * step : (i + 1) * step], piece)
-        loss, part = negative_pairs(low_a, low(late), scale_value, bias_value)
+        one = jnp.where(inner | end, held[a:b], low(relayed))
+        loss, part = negative_pairs(low_a, one, scale_value, bias_value)
         grad_a, loss_a = grad_a + part, loss_a + loss
     out_a = unit_backward(grad_a, unit_a, factor_a)
 

time: 280 us -> 224 us (0.80)
  the two profiles are of different devices: /device:TPU:32 before, /device:TPU:8 now
where the time goes in v2:
time: 224 us; the launch traced here: 223 us
  waiting for transfers between devices  146 us (65%)
  starting transfers between devices  52.2 us (23%)
  matrix products  12.3 us (5%)
  other arithmetic  10.5 us (5%)
    ppermute x1, waiting for transfers between devices, shards(): far = [lax.ppermute(raw_a[a:b], AXES, far_pairs) for a, b in PARTS]  131 us
    ppermute x1, starting transfers between devices, shards(): far = [lax.ppermute(raw_a[a:b], AXES, far_pairs) for a, b in PARTS]  32.3 us
    ppermute x1, waiting for transfers between devices, shards(): moved = lax.ppermute(piece, AXES, shift_pairs)  15 us
    ppermute x1, starting transfers between devices, shards(): moved = lax.ppermute(piece, AXES, shift_pairs)  8.9 us
    dot_general x5, matrix products, logits_of(): jnp.einsum('id,jd->ij', rows, columns, preferred_element_type=jnp.float32)  6.5 us
    dot_general x5, matrix products, apply(): jnp.einsum('ij,jd->id', weights, values, preferred_element_type=jnp.float32)  4.94 us
    ppermute x1, starting transfers between devices, shards(): middle = lax.ppermute(jnp.where(inner, low_b, low_a), AXES, middle_pairs)  4.69 us
    ppermute x2, starting transfers between devices, within(): return lax.ppermute(value, AXES, pairs)  4.69 us
  transfers between devices with their start and end apart: 6, of which 2 were waited for; matrix products, arithmetic and copies ran while one was open for 5% of the time, Pallas kernels for 0%

profile of v2, /device:TPU:8, one launch (start us, length us, event | category | flops | bytes accessed | tf_op | source)
XLA Modules:
  0.0 223.4 jit_solution(14704761860078232671)
XLA Ops:
  0.6 2.3 %fusion.15 = (f32[384]{0:T(512)S(1)}, bf16[384,1152]{1,0:T(8,128)(2,1)S(1)}, f32[384]{0:T(512)S(1)}, bf16[384,1152]{1,0:T(8,128)(2,1)S(1)}) fusion(bf16[384,1152]{1,0:T(8,128)(2,1)} %param.5, bf16[384,1152]{1,0:T(8,128)(2,1)} %param.4, pred[]{:T(512)S(6)} %lt.16), kind=kLoop, calls=%fused_computation.27 | loop fusion | flops 3538176 | bytes 3542017 | tf_op jit(solution)/shard_map/reduce_sum | solution.py:47
  3.0 32.3 %collective-permute-start = (bf16[384,1152]{1,0:T(8,128)(2,1)S(1)}, bf16[384,1152]{1,0:T(8,128)(2,1)}, u32[]{:S(2)}, u32[]{:S(2)}) collective-permute-start(bf16[384,1152]{1,0:T(8,128)(2,1)S(1)} %get-tuple-element.17), channel_id=1, source_target_pairs={{2,4},{3,5},{0,62},{1,63},{6,8},{7,9},{4,2},{5,3},{10,12},{11,13},... | collective-permute-start | bytes 2654216 | tf_op jit(solution)/shard_map/ppermute | solution.py:89
  35.4 1.3 broadcast_select_fusion.2
  36.7 1.9 collective-permute-start.5
  38.6 1.2 broadcast_select_fusion.1
  39.9 4.7 %collective-permute-start.3 = (bf16[384,1152]{1,0:T(8,128)(2,1)}, bf16[384,1152]{1,0:T(8,128)(2,1)S(1)}, u32[]{:S(2)}, u32[]{:S(2)}) collective-permute-start(bf16[384,1152]{1,0:T(8,128)(2,1)} %broadcast_select_fusion.1), channel_id=1, source_target_pairs={{0,1023},{1023,0},{1,2},{2,1},{5,6},{6,5},{9,10},{10,9},{13,14},{1... | collective-permute-start | bytes 2654216 | tf_op jit(solution)/shard_map/ppermute | solution.py:95
  44.6 2.8 %collective-permute-start.2 = (bf16[384,1152]{1,0:T(8,128)(2,1)}, bf16[384,1152]{1,0:T(8,128)(2,1)}, u32[]{:S(2)}, u32[]{:S(2)}) collective-permute-start(bf16[384,1152]{1,0:T(8,128)(2,1)} %get-tuple-element.10), channel_id=1, source_target_pairs={{0,1},{1,0},{2,3},{3,2},{4,5},{5,4},{6,7},{7,6},{8,9},{9,8},{10,11... | collective-permute-start | bytes 2654216 | tf_op jit(solution)/shard_map/ppermute | solution.py:42
  48.7 1.1 fusion.41
  49.8 0.7 fusion.48
  50.5 0.8 fusion.47
  51.3 131.4 %collective-permute-done = bf16[384,1152]{1,0:T(8,128)(2,1)} collective-permute-done((bf16[384,1152]{1,0:T(8,128)(2,1)S(1)}, bf16[384,1152]{1,0:T(8,128)(2,1)}, u32[]{:S(2)}, u32[]{:S(2)}) %collective-permute-start) | collective-permute-done | bytes 884768 | tf_op jit(solution)/shard_map/ppermute | solution.py:89
  182.7 8.9 %collective-permute-start.1 = (bf16[384,1152]{1,0:T(8,128)(2,1)}, bf16[384,1152]{1,0:T(8,128)(2,1)S(1)}, u32[]{:S(2)}, u32[]{:S(2)}) collective-permute-start(bf16[384,1152]{1,0:T(8,128)(2,1)} %collective-permute-done), channel_id=1, source_target_pairs={{62,1022},{63,1023},{0,64},{1,65},{126,62},{127,63},{64,128},{65,1... | collective-permute-start | bytes 2654216 | tf_op jit(solution)/shard_map/ppermute | solution.py:116
  191.6 1.5 collective-permute-start.4
  193.1 0.0 collective-permute-done.3
  193.1 0.0 collective-permute-done.2
  193.1 1.0 fusion.30
  194.2 0.0 collective-permute-done.5
  194.2 2.2 fusion.29
  196.4 1.8 convolution_add_fusion.1
  198.2 0.9 fusion.11
  199.1 15.0 %collective-permute-done.1 = bf16[384,1152]{1,0:T(8,128)(2,1)S(1)} collective-permute-done((bf16[384,1152]{1,0:T(8,128)(2,1)}, bf16[384,1152]{1,0:T(8,128)(2,1)S(1)}, u32[]{:S(2)}, u32[]{:S(2)}) %collective-permute-start.1) | collective-permute-done | bytes 884768 | tf_op jit(solution)/shard_map/ppermute | solution.py:116
  214.0 0.4 fusion.16
  214.4 0.0 collective-permute-done.4
  214.4 0.3 fusion.18
  214.7 1.1 fusion.27
  215.8 0.8 convolution_add_fusion.3
  216.6 1.6 fusion.26
  218.2 1.0 fusion.28
  219.2 0.8 fusion.6
  220.1 1.7 broadcast_select_fusion.4
  221.8 1.0 broadcast_select_fusion.5
  222.8 0.6 add_multiply_fusion
  (3 shorter events, 0.0 us)
Async XLA Ops:
  3.0 179.7 %collective-permute-start = (bf16[384,1152]{1,0:T(8,128)(2,1)S(1)}, bf16[384,1152]{1,0:T(8,128)(2,1)}, u32[]{:S(2)}, u32[]{:S(2)}) collective-permute-start(bf16[384,1152]{1,0:T(8,128)(2,1)S(1)} %get-tuple-element.17), channel_id=1, source_target_pairs={{2,4},{3,5},{0,62},{1,63},{6,8},{7,9},{4,2},{5,3},{10,12},{11,13},... | collective-permute-start | bytes 2654216 | tf_op jit(solution)/shard_map/ppermute | solution.py:89
  36.7 157.5 %collective-permute-start.5 = (bf16[384,1152]{1,0:T(8,128)(2,1)S(1)}, bf16[384,1152]{1,0:T(8,128)(2,1)}, u32[]{:S(2)}, u32[]{:S(2)}) collective-permute-start(bf16[384,1152]{1,0:T(8,128)(2,1)S(1)} %get-tuple-element.11), channel_id=1, source_target_pairs={{0,2},{1,3},{2,0},{3,1},{4,6},{5,7},{6,4},{7,5},{8,10},{9,11},{10,... | collective-permute-start | bytes 2654216 | tf_op jit(solution)/shard_map/ppermute | solution.py:42
  39.9 153.3 %collective-permute-start.3 = (bf16[384,1152]{1,0:T(8,128)(2,1)}, bf16[384,1152]{1,0:T(8,128)(2,1)S(1)}, u32[]{:S(2)}, u32[]{:S(2)}) collective-permute-start(bf16[384,1152]{1,0:T(8,128)(2,1)} %broadcast_select_fusion.1), channel_id=1, source_target_pairs={{0,1023},{1023,0},{1,2},{2,1},{5,6},{6,5},{9,10},{10,9},{13,14},{1... | collective-permute-start | bytes 2654216 | tf_op jit(solution)/shard_map/ppermute | solution.py:95
  44.6 148.6 %collective-permute-start.2 = (bf16[384,1152]{1,0:T(8,128)(2,1)}, bf16[384,1152]{1,0:T(8,128)(2,1)}, u32[]{:S(2)}, u32[]{:S(2)}) collective-permute-start(bf16[384,1152]{1,0:T(8,128)(2,1)} %get-tuple-element.10), channel_id=1, source_target_pairs={{0,1},{1,0},{2,3},{3,2},{4,5},{5,4},{6,7},{7,6},{8,9},{9,8},{10,11... | collective-permute-start | bytes 2654216 | tf_op jit(solution)/shard_map/ppermute | solution.py:42
  182.7 31.4 %collective-permute-start.1 = (bf16[384,1152]{1,0:T(8,128)(2,1)}, bf16[384,1152]{1,0:T(8,128)(2,1)S(1)}, u32[]{:S(2)}, u32[]{:S(2)}) collective-permute-start(bf16[384,1152]{1,0:T(8,128)(2,1)} %collective-permute-done), channel_id=1, source_target_pairs={{62,1022},{63,1023},{0,64},{1,65},{126,62},{127,63},{64,128},{65,1... | collective-permute-start | bytes 2654216 | tf_op jit(solution)/shard_map/ppermute | solution.py:116
  191.6 22.9 %collective-permute-start.4 = (bf16[384,1152]{1,0:T(8,128)(2,1)}, bf16[384,1152]{1,0:T(8,128)(2,1)S(1)}, u32[]{:S(2)}, u32[]{:S(2)}) collective-permute-start(bf16[384,1152]{1,0:T(8,128)(2,1)} %collective-permute-done), channel_id=1, source_target_pairs={{5,4},{9,8},{2,3},{13,12},{6,7},{17,16},{10,11},{21,20},{14,15},{2... | collective-permute-start | bytes 2654216 | tf_op jit(solution)/shard_map/ppermute | solution.py:117

commit v3 on v2

--- a/solution.py
+++ b/solution.py
@@ -1,17 +1,20 @@
 import jax
 import jax.numpy as jnp
 from jax import lax
+from jax.experimental import pallas as pl
+from jax.experimental.pallas import tpu as pltpu
 from jax.sharding import PartitionSpec as P
 
 AXES = ("dp", "group")
 RUN = 4
 LAYER = 16
-PARTS = ((0, 384),)
+ROW_STEP = 128
+LANES = 128
 
 
 def tables(count):
     runs = count // RUN
-    far, shift, relay = [], [], []
+    far, shift, relay, wrap = [], [], [], []
     middle = [(0, count - 1), (count - 1, 0)]
     for run in range(runs):
         middle += [(run * RUN + 1, run * RUN + 2), (run * RUN + 2, run * RUN + 1)]
@@ -19,19 +22,23 @@
         slot = (run + 1 - (LAYER if step else 0)) % runs
         final = (run + 1) % runs
         far += [(run * RUN + y, slot * RUN + y - 2) for y in (2, 3)]
-        if step:
-            shift += [(slot * RUN + y, final * RUN + y) for y in (0, 1)]
-        if final != 0:
+        if final == 0:
+            wrap += [(run * RUN + y, final * RUN + y - 2) for y in (2, 3)]
+        else:
+            if step:
+                shift += [(slot * RUN + y, final * RUN + y) for y in (0, 1)]
             relay += [(slot * RUN + 1, final * RUN)]
         step = run % LAYER == 0
         slot = (run - 1 + (LAYER if step else 0)) % runs
         final = (run - 1) % runs
         far += [(run * RUN + y, slot * RUN + y + 2) for y in (0, 1)]
-        if step:
-            shift += [(slot * RUN + y, final * RUN + y) for y in (2, 3)]
-        if run != 0:
+        if run == 0:
+            wrap += [(run * RUN + y, final * RUN + y + 2) for y in (0, 1)]
+        else:
+            if step:
+                shift += [(slot * RUN + y, final * RUN + y) for y in (2, 3)]
             relay += [(slot * RUN + 2, final * RUN + 3)]
-    return far, shift, relay, middle
+    return far, shift, relay, middle, wrap
 
 
 def within(value, hops):
@@ -71,6 +78,74 @@
     losses = jnp.sum(jax.nn.softplus(logits), axis=1)
     weights = (scale_value * jax.nn.sigmoid(logits)).astype(jnp.bfloat16)
     return losses, apply(weights, columns)
+
+
+def finish_kernel(
+    choices, constants, relayed, held, low_a, raw_a, factor_a, grad_a, out_b, before, loss_out, image_out, text_out, one
+):
+    rows = low_a.shape[0]
+    scale_value, bias_value = constants[0], constants[1]
+    use_held, first_half = choices[0] == 1, choices[1] == 1
+
+    @pl.when(use_held)
+    def _():
+        one[...] = held[...]
+
+    @pl.when(jnp.logical_not(use_held))
+    def _():
+        for start in range(0, rows, ROW_STEP):
+            at = pl.ds(start, ROW_STEP)
+            one[at, :] = low(relayed[at, :])
+
+    def last_rows(a_out, b_out, is_image):
+        for start in range(0, rows, ROW_STEP):
+            at = pl.ds(start, ROW_STEP)
+            dots = lax.dot_general(
+                low_a[at, :], one[...], (((1,), (1,)), ((), ())), preferred_element_type=jnp.float32
+            )
+            logits = scale_value * dots + bias_value
+            weights = (scale_value * jax.nn.sigmoid(logits)).astype(jnp.bfloat16)
+            part = jnp.dot(weights, one[...], preferred_element_type=jnp.float32)
+            factor = factor_a[at, 0:1]
+            unit = raw_a[at, :].astype(jnp.float32) * factor
+            a_out[at, :] = unit_backward(grad_a[at, :] + part, unit, factor)
+            b_out[at, :] = out_b[at, :]
+            total = before[:, at]
+            if is_image:
+                plus = jnp.maximum(logits, 0.0) + jnp.log1p(jnp.exp(-jnp.abs(logits)))
+                losses = jnp.sum(plus, axis=1, keepdims=True)
+                total = total + jnp.broadcast_to(losses, (ROW_STEP, ROW_STEP)).T[0:1, :]
+            loss_out[:, at] = total / (3.0 * rows)
+
+    @pl.when(first_half)
+    def _():
+        last_rows(image_out, text_out, True)
+
+    @pl.when(jnp.logical_not(first_half))
+    def _():
+        last_rows(text_out, image_out, False)
+
+
+def finish(choices, constants, relayed, held, low_a, raw_a, factor_a, grad_a, out_b, before):
+    rows, features = low_a.shape
+    vmem = pl.BlockSpec(memory_space=pltpu.VMEM)
+    smem = pl.BlockSpec(memory_space=pltpu.SMEM)
+    loss, image_grad, text_grad = pl.pallas_call(
+        finish_kernel,
+        out_shape=(
+            jax.ShapeDtypeStruct((1, rows), jnp.float32),
+            jax.ShapeDtypeStruct((rows, features), jnp.bfloat16),
+            jax.ShapeDtypeStruct((rows, features), jnp.bfloat16),
+        ),
+        in_specs=[smem] * 2 + [vmem] * 8,
+        out_specs=(vmem,) * 3,
+        scratch_shapes=[pltpu.VMEM((rows, features), jnp.bfloat16)],
+        compiler_params=pltpu.CompilerParams(vmem_limit_bytes=24 * 1024 * 1024),
+        cost_estimate=pl.CostEstimate(
+            flops=4 * rows * rows * features, bytes_accessed=8 * rows * features, transcendentals=3 * rows * rows
+        ),
+    )(choices, constants, relayed, held, low_a, raw_a, factor_a, grad_a, out_b, before.reshape(1, rows))
+    return (loss.reshape(rows), image_grad, text_grad)
 
 
 def shards(images, texts, logit_scale, logit_bias):
@@ -83,15 +158,17 @@
     inner = (place == 1) | (place == 2)
     shifted = jnp.where(first_half, run % LAYER == 0, run % LAYER == LAYER - 1)
     end = (index == 0) | (index == count - 1)
-    far_pairs, shift_pairs, relay_pairs, middle_pairs = tables(count)
-    raw_a = jnp.where(first_half, images, texts)
+    wrapped = jnp.where(first_half, run == 0, run == count // RUN - 1)
+    far_pairs, shift_pairs, relay_pairs, middle_pairs, wrap_pairs = tables(count)
+    raw_a = lax.optimization_barrier(jnp.where(first_half, images, texts))
     raw_b = jnp.where(first_half, texts, images)
-    far = [lax.ppermute(raw_a[a:b], AXES, far_pairs) for a, b in PARTS]
+    far = lax.ppermute(raw_a, AXES, far_pairs)
     unit_a, factor_a = normalize(raw_a)
     unit_b, factor_b = normalize(raw_b)
     low_a, low_b = unit_a.astype(jnp.bfloat16), unit_b.astype(jnp.bfloat16)
     near_two = within(low_b, {0: 2, 2: 0, 1: 3, 3: 1})
     near_one = within(jnp.where(inner, low_a, low_b), {1: 0, 2: 3, 0: 1, 3: 2})
+    wrap = lax.ppermute(low_a, AXES, wrap_pairs)
     middle = lax.ppermute(jnp.where(inner, low_b, low_a), AXES, middle_pairs)
 
     labels = 2.0 * jnp.eye(count_rows, dtype=jnp.float32) - 1.0
@@ -102,8 +179,12 @@
     grad_a = apply(weights, low_b)
     grad_b = jnp.einsum("ij,id->jd", weights, low_a, preferred_element_type=jnp.float32)
 
+    relayed = lax.ppermute(far, AXES, relay_pairs)
+
     loss_two, part = negative_pairs(low_b, near_two, scale_value, bias_value)
     grad_b = grad_b + part
+    shift_from, loss_two = lax.optimization_barrier((far, loss_two))
+    moved = lax.ppermute(shift_from, AXES, shift_pairs)
     early = jnp.where(inner, middle, near_one)
     loss_one, part = negative_pairs(low_b, early, scale_value, bias_value)
     grad_b = grad_b + part
@@ -111,20 +192,14 @@
     loss_b = loss_two + loss_one
 
     held = jnp.where(inner, near_one, middle)
-    loss_a = jnp.zeros_like(loss_b)
-    for (a, b), piece in zip(PARTS, far):
-        moved = lax.ppermute(piece, AXES, shift_pairs)
-        relayed = lax.ppermute(piece, AXES, relay_pairs)
-        two = low(jnp.where(shifted, moved, piece))
-        loss, part = negative_pairs(low_a, two, scale_value, bias_value)
-        grad_a, loss_a = grad_a + part, loss_a + loss
-        one = jnp.where(inner | end, held[a:b], low(relayed))
-        loss, part = negative_pairs(low_a, one, scale_value, bias_value)
-        grad_a, loss_a = grad_a + part, loss_a + loss
-    out_a = unit_backward(grad_a, unit_a, factor_a)
-
-    row_loss = (own_loss + jnp.where(first_half, loss_a, loss_b)) / (3.0 * count_rows)
-    return (row_loss, jnp.where(first_half, out_a, out_b), jnp.where(first_half, out_b, out_a))
+    two = jnp.where(wrapped, wrap, low(jnp.where(shifted, moved, far)))
+    loss_a, part = negative_pairs(low_a, two, scale_value, bias_value)
+    grad_a = grad_a + part
+    before = own_loss + jnp.where(first_half, loss_a, loss_b)
+    choices = jnp.stack([inner | end, first_half]).astype(jnp.int32)
+    constants = jnp.stack([scale_value, bias_value])
+    factor_wide = jnp.broadcast_to(factor_a, (count_rows, LANES))
+    return finish(choices, constants, relayed, held, low_a, raw_a, factor_wide, grad_a, out_b, before)
 
 
 def solution(mesh):

time: 224 us -> 220 us (0.982)
  the two profiles are of different devices: /device:TPU:8 before, /device:TPU:96 now
where the time goes in v3:
time: 220 us; the launch traced here: 219 us
  waiting for transfers between devices  147 us (67%)
  starting transfers between devices  40.8 us (19%)
  matrix products  15.3 us (7%)
  other arithmetic  9.19 us (4%)
  Pallas kernels  4.65 us (2%)
    ppermute x1, waiting for transfers between devices, shards(): far = lax.ppermute(raw_a, AXES, far_pairs)  125 us
    ppermute x1, starting transfers between devices, shards(): far = lax.ppermute(raw_a, AXES, far_pairs)  30.5 us
    ppermute x2, waiting for transfers between devices, within(): return lax.ppermute(value, AXES, pairs)  11.9 us
    dot_general x4, matrix products, logits_of(): jnp.einsum('id,jd->ij', rows, columns, preferred_element_type=jnp.float32)  8.19 us
    ppermute x1, waiting for transfers between devices, shards(): relayed = lax.ppermute(far, AXES, relay_pairs)  6.9 us
    dot_general x4, matrix products, apply(): jnp.einsum('ij,jd->id', weights, values, preferred_element_type=jnp.float32)  6.38 us
    pallas_call x1, Pallas kernels, finish(): pl.pallas_call(finish_kernel, out_shape=(jax.ShapeDtypeStruct((1, rows),...  4.65 us
  transfers between devices with their start and end apart: 7, of which 4 were waited for; matrix products, arithmetic and copies ran while one was open for 10% of the time, Pallas kernels for 0%

profile of v3, /device:TPU:96, one launch (start us, length us, event | category | flops | bytes accessed | tf_op | source)
XLA Modules:
  0.0 219.2 jit_solution(1997878024683098801)
XLA Ops:
  0.6 0.0 copy-start
  0.7 0.0 copy-start.1
  0.7 1.4 broadcast_select_fusion.6.raw_a
  2.1 30.5 %collective-permute-start = (bf16[384,1152]{1,0:T(8,128)(2,1)S(1)}, bf16[384,1152]{1,0:T(8,128)(2,1)S(1)}, u32[]{:S(2)}, u32[]{:S(2)}) collective-permute-start(bf16[384,1152]{1,0:T(8,128)(2,1)S(1)} %broadcast_select_fusion.6.raw_a), channel_id=1, source_target_pairs={{2,4},{3,5},{0,62},{1,63},{6,8},{7,9},{4,2},{5,3},{10,12},{11,13},... | collective-permute-start | bytes 2654216 | tf_op jit(solution)/shard_map/ppermute | solution.py:165
  32.6 0.0 copy-done
  32.6 0.0 copy-done.1
  32.6 0.4 fusion.9
  33.1 0.3 fusion.3
  33.3 1.7 broadcast_select_fusion.3
  35.0 1.9 collective-permute-start.5
  36.9 1.6 collective-permute-start.4
  38.5 2.2 broadcast_select_fusion.4
  40.7 1.9 collective-permute-start.2
  42.6 1.6 collective-permute-start.3
  45.5 0.1 pad_maximum_fusion.constants
  45.6 0.1 add_convert_fusion.choices
  45.7 2.2 %fusion.27 = (f32[384]{0:T(512)S(1)}, f32[384]{0:T(512)S(1)}, f32[384,384]{1,0:T(8,128)S(1)}) fusion(f32[]{:T(128)} %bitcast.23, bf16[384,1152]{1,0:T(8,128)(2,1)S(1)} %get-tuple-element.17.low_a, bf16[384,1152]{1,0:T(8,128)(2,1)} %get-tuple-element.16, f32[]{:T(128)} %bitcast.16), kind=kOutput, calls=%fused_computation.57 | convolution fusion | flops 341949696 | bytes 2362376 | tf_op jit(solution)/shard_map/id,jd->ij/dot_general | solution.py:68
  47.9 0.7 fusion.32
  48.6 1.8 fusion.33
  50.5 11.9 %collective-permute-done.5 = bf16[384,1152]{1,0:T(8,128)(2,1)} collective-permute-done((bf16[384,1152]{1,0:T(8,128)(2,1)}, bf16[384,1152]{1,0:T(8,128)(2,1)}, u32[]{:S(2)}, u32[]{:S(2)}) %collective-permute-start.5) | collective-permute-done | bytes 884768 | tf_op jit(solution)/shard_map/ppermute | solution.py:49
  62.3 2.4 %fusion.18 = (f32[384]{0:T(512)S(1)}, f32[384,384]{1,0:T(8,128)S(1)}) fusion(f32[]{:T(128)} %bitcast.26, bf16[384,1152]{1,0:T(8,128)(2,1)} %get-tuple-element.16, bf16[384,1152]{1,0:T(8,128)(2,1)} %collective-permute-done.5, f32[]{:T(128)} %bitcast.22), kind=kOutput, calls=%fused_computation.42 | convolution fusion | flops 341065344 | bytes 2360840 | tf_op jit(solution)/shard_map/id,jd->ij/dot_general | solution.py:68
  64.8 124.7 %collective-permute-done = bf16[384,1152]{1,0:T(8,128)(2,1)S(1)} collective-permute-done((bf16[384,1152]{1,0:T(8,128)(2,1)S(1)}, bf16[384,1152]{1,0:T(8,128)(2,1)S(1)}, u32[]{:S(2)}, u32[]{:S(2)}) %collective-permute-start) | collective-permute-done | bytes 884768 | tf_op jit(solution)/shard_map/ppermute | solution.py:165
  189.4 1.9 collective-permute-start.6
  191.4 1.3 collective-permute-start.1
  192.7 1.8 convolution_add_fusion.1
  194.5 0.0 collective-permute-done.2
  194.5 0.0 collective-permute-done.3
  194.5 2.5 %fusion.20 = (f32[384]{0:T(512)S(1)}, f32[384,384]{1,0:T(8,128)S(1)}) fusion(f32[]{:T(128)} %bitcast.24, bf16[384,1152]{1,0:T(8,128)(2,1)} %get-tuple-element.16, bf16[384,1152]{1,0:T(8,128)(2,1)} %collective-permute-done.3, bf16[384,1152]{1,0:T(8,128)(2,1)} %collective-permute-done.2, pred[]{:T(512)S(6)} %or.9, f32[]{:T(128)} %bitcast.18), kind=kOutput, calls=%fused_computation.44 | convolution fusion | flops 341507712 | bytes 3245577 | tf_op jit(solution)/shard_map/id,jd->ij/dot_general | solution.py:68
  197.0 2.1 fusion.5
  199.0 0.4 fusion.8.out_b
  199.5 1.3 broadcast_select_fusion.2.held
  200.7 3.6 %collective-permute-done.6 = bf16[384,1152]{1,0:T(8,128)(2,1)S(1)} collective-permute-done((bf16[384,1152]{1,0:T(8,128)(2,1)S(1)}, bf16[384,1152]{1,0:T(8,128)(2,1)S(1)}, u32[]{:S(2)}, u32[]{:S(2)}) %collective-permute-start.6) | collective-permute-done | bytes 884768 | tf_op jit(solution)/shard_map/ppermute | solution.py:187
  204.4 0.4 fusion.10
  204.8 0.0 collective-permute-done.4
  204.8 0.4 fusion.17
  205.2 1.0 fusion.19
  206.2 0.7 convolution_add_fusion.2.grad_a
  206.9 6.9 %collective-permute-done.1.relayed = bf16[384,1152]{1,0:T(8,128)(2,1)S(1)} collective-permute-done((bf16[384,1152]{1,0:T(8,128)(2,1)S(1)}, bf16[384,1152]{1,0:T(8,128)(2,1)S(1)}, u32[]{:S(2)}, u32[]{:S(2)}) %collective-permute-start.1) | collective-permute-done | bytes 884768 | tf_op jit(solution)/shard_map/ppermute | solution.py:182
  213.8 0.1 broadcast_in_dim.2.factor_a
  213.9 4.7 %shard_map.67 = (f32[1,384]{1,0:T(1,128)S(1)}, bf16[384,1152]{1,0:T(8,128)(2,1)}, bf16[384,1152]{1,0:T(8,128)(2,1)}) custom-call(s32[2]{0:T(128)S(1)} %add_convert_fusion.choices, f32[2]{0:T(128)S(1)} %pad_maximum_fusion.constants, bf16[384,1152]{1,0:T(8,128)(2,1)S(1)} %collective-permute-done.1.relayed, bf16[384,1152]{1,0:T(8,128)(2,1)S(1)} %broadcast_select_fusion.2.held, ...), custom_call_target="tpu_custom_call" | custom-call | flops 679477248 | bytes 3538944 | tf_op jit(solution)/shard_map/pallas_call | solution.py:133
  218.6 0.6 reduce
  (4 shorter events, 0.0 us)
Async XLA Ops:
  0.6 32.0 %copy-start = (bf16[384,1152]{1,0:T(8,128)(2,1)S(1)}, bf16[384,1152]{1,0:T(8,128)(2,1)}, u32[]{:S(2)}) copy-start(bf16[384,1152]{1,0:T(8,128)(2,1)} %param.4) | copy-start | bytes 2654212
  0.7 32.0 %copy-start.1 = (bf16[384,1152]{1,0:T(8,128)(2,1)S(1)}, bf16[384,1152]{1,0:T(8,128)(2,1)}, u32[]{:S(2)}) copy-start(bf16[384,1152]{1,0:T(8,128)(2,1)} %param.5) | copy-start | bytes 2654212
  2.1 187.4 %collective-permute-start = (bf16[384,1152]{1,0:T(8,128)(2,1)S(1)}, bf16[384,1152]{1,0:T(8,128)(2,1)S(1)}, u32[]{:S(2)}, u32[]{:S(2)}) collective-permute-start(bf16[384,1152]{1,0:T(8,128)(2,1)S(1)} %broadcast_select_fusion.6.raw_a), channel_id=1, source_target_pairs={{2,4},{3,5},{0,62},{1,63},{6,8},{7,9},{4,2},{5,3},{10,12},{11,13},... | collective-permute-start | bytes 2654216 | tf_op jit(solution)/shard_map/ppermute | solution.py:165
  35.0 27.3 %collective-permute-start.5 = (bf16[384,1152]{1,0:T(8,128)(2,1)}, bf16[384,1152]{1,0:T(8,128)(2,1)}, u32[]{:S(2)}, u32[]{:S(2)}) collective-permute-start(bf16[384,1152]{1,0:T(8,128)(2,1)} %get-tuple-element.16), channel_id=1, source_target_pairs={{0,2},{1,3},{2,0},{3,1},{4,6},{5,7},{6,4},{7,5},{8,10},{9,11},{10,... | collective-permute-start | bytes 2654216 | tf_op jit(solution)/shard_map/ppermute | solution.py:49
  36.9 167.8 %collective-permute-start.4 = (bf16[384,1152]{1,0:T(8,128)(2,1)S(1)}, bf16[384,1152]{1,0:T(8,128)(2,1)}, u32[]{:S(2)}, u32[]{:S(2)}) collective-permute-start(bf16[384,1152]{1,0:T(8,128)(2,1)S(1)} %get-tuple-element.17.low_a), channel_id=1, source_target_pairs={{0,1022},{1,1023},{1022,0},{1023,1}} | collective-permute-start | bytes 2654216 | tf_op jit(solution)/shard_map/ppermute | solution.py:171
  40.7 153.8 %collective-permute-start.2 = (bf16[384,1152]{1,0:T(8,128)(2,1)}, bf16[384,1152]{1,0:T(8,128)(2,1)}, u32[]{:S(2)}, u32[]{:S(2)}) collective-permute-start(bf16[384,1152]{1,0:T(8,128)(2,1)} %broadcast_select_fusion.4), channel_id=1, source_target_pairs={{0,1},{1,0},{2,3},{3,2},{4,5},{5,4},{6,7},{7,6},{8,9},{9,8},{10,11... | collective-permute-start | bytes 2654216 | tf_op jit(solution)/shard_map/ppermute | solution.py:49
  42.6 151.9 %collective-permute-start.3 = (bf16[384,1152]{1,0:T(8,128)(2,1)}, bf16[384,1152]{1,0:T(8,128)(2,1)}, u32[]{:S(2)}, u32[]{:S(2)}) collective-permute-start(bf16[384,1152]{1,0:T(8,128)(2,1)} %get-tuple-element.15), channel_id=1, source_target_pairs={{0,1023},{1023,0},{1,2},{2,1},{5,6},{6,5},{9,10},{10,9},{13,14},{1... | collective-permute-start | bytes 2654216 | tf_op jit(solution)/shard_map/ppermute | solution.py:172
  189.4 14.9 %collective-permute-start.6 = (bf16[384,1152]{1,0:T(8,128)(2,1)S(1)}, bf16[384,1152]{1,0:T(8,128)(2,1)S(1)}, u32[]{:S(2)}, u32[]{:S(2)}) collective-permute-start(bf16[384,1152]{1,0:T(8,128)(2,1)S(1)} %collective-permute-done), channel_id=1, source_target_pairs={{0,64},{1,65},{126,62},{127,63},{64,128},{65,129},{190,126},{191,1... | collective-permute-start | bytes 2654216 | tf_op jit(solution)/shard_map/ppermute | solution.py:187
  191.4 22.5 %collective-permute-start.1 = (bf16[384,1152]{1,0:T(8,128)(2,1)S(1)}, bf16[384,1152]{1,0:T(8,128)(2,1)S(1)}, u32[]{:S(2)}, u32[]{:S(2)}) collective-permute-start(bf16[384,1152]{1,0:T(8,128)(2,1)S(1)} %collective-permute-done), channel_id=1, source_target_pairs={{5,4},{9,8},{2,3},{13,12},{6,7},{17,16},{10,11},{21,20},{14,15},{2... | collective-permute-start | bytes 2654216 | tf_op jit(solution)/shard_map/ppermute | solution.py:182

commit v4 on v3

--- a/solution.py
+++ b/solution.py
@@ -179,20 +179,21 @@
     grad_a = apply(weights, low_b)
     grad_b = jnp.einsum("ij,id->jd", weights, low_a, preferred_element_type=jnp.float32)
 
-    relayed = lax.ppermute(far, AXES, relay_pairs)
 
     loss_two, part = negative_pairs(low_b, near_two, scale_value, bias_value)
     grad_b = grad_b + part
-    shift_from, loss_two = lax.optimization_barrier((far, loss_two))
-    moved = lax.ppermute(shift_from, AXES, shift_pairs)
     early = jnp.where(inner, middle, near_one)
     loss_one, part = negative_pairs(low_b, early, scale_value, bias_value)
     grad_b = grad_b + part
     out_b = unit_backward(grad_b, unit_b, factor_b)
     loss_b = loss_two + loss_one
+    far, loss_b = lax.optimization_barrier((far, loss_b))
+    relayed = lax.ppermute(far, AXES, relay_pairs)
+    shift_from, low_far = lax.optimization_barrier((far, low(far)))
+    moved = lax.ppermute(shift_from, AXES, shift_pairs)
 
     held = jnp.where(inner, near_one, middle)
-    two = jnp.where(wrapped, wrap, low(jnp.where(shifted, moved, far)))
+    two = jnp.where(wrapped, wrap, jnp.where(shifted, low(moved), low_far))
     loss_a, part = negative_pairs(low_a, two, scale_value, bias_value)
     grad_a = grad_a + part
     before = own_loss + jnp.where(first_half, loss_a, loss_b)

time: 220 us -> 232 us (1.055)
  the two profiles are of different devices: /device:TPU:96 before, /device:TPU:32 now
where the time goes in v4:
time: 232 us
  waiting for transfers between devices  155 us (67%)
  starting transfers between devices  46.4 us (20%)
  matrix products  12.6 us (5%)
  other arithmetic  10.5 us (5%)
  Pallas kernels  4.64 us (2%)
    ppermute x1, waiting for transfers between devices, shards(): far = lax.ppermute(raw_a, AXES, far_pairs)  104 us
    ppermute x1, starting transfers between devices, shards(): far = lax.ppermute(raw_a, AXES, far_pairs)  32.3 us
    ppermute x1, waiting for transfers between devices, shards(): moved = lax.ppermute(shift_from, AXES, shift_pairs)  26 us
    ppermute x2, waiting for transfers between devices, within(): return lax.ppermute(value, AXES, pairs)  24.9 us
    ppermute x2, starting transfers between devices, within(): return lax.ppermute(value, AXES, pairs)  7.62 us
    dot_general x4, matrix products, logits_of(): jnp.einsum('id,jd->ij', rows, columns, preferred_element_type=jnp.float32)  6.36 us
    dot_general x4, matrix products, apply(): jnp.einsum('ij,jd->id', weights, values, preferred_element_type=jnp.float32)  5.57 us
    pallas_call x1, Pallas kernels, finish(): pl.pallas_call(finish_kernel, out_shape=(jax.ShapeDtypeStruct((1, rows),...  4.64 us
  transfers between devices with their start and end apart: 7, of which 4 were waited for; matrix products, arithmetic and copies ran while one was open for 9% of the time, Pallas kernels for 0%

profile of v4, /device:TPU:32, one launch (start us, length us, event | category | flops | bytes accessed | tf_op | source)
XLA Modules:
  0.0 231.7 jit_solution(14531663177047962922)
XLA Ops:
  0.6 0.0 copy-start
  0.6 0.0 copy-start.1
  0.7 1.4 broadcast_select_fusion.5.raw_a
  2.1 32.3 %collective-permute-start = (bf16[384,1152]{1,0:T(8,128)(2,1)S(1)}, bf16[384,1152]{1,0:T(8,128)(2,1)}, u32[]{:S(2)}, u32[]{:S(2)}) collective-permute-start(bf16[384,1152]{1,0:T(8,128)(2,1)S(1)} %broadcast_select_fusion.5.raw_a), channel_id=1, source_target_pairs={{2,4},{3,5},{0,62},{1,63},{6,8},{7,9},{4,2},{5,3},{10,12},{11,13},... | collective-permute-start | bytes 2654216 | tf_op jit(solution)/shard_map/ppermute | solution.py:165
  34.4 0.0 copy-done
  34.4 0.0 copy-done.1
  34.4 0.4 fusion.7
  34.8 0.3 fusion.8
  35.1 1.4 broadcast_select_fusion.2
  36.5 1.9 collective-permute-start.1
  38.4 1.6 collective-permute-start.5
  40.0 1.0 broadcast_select_fusion.3
  41.1 1.6 collective-permute-start.2
  42.6 5.7 %collective-permute-start.3 = (bf16[384,1152]{1,0:T(8,128)(2,1)}, bf16[384,1152]{1,0:T(8,128)(2,1)}, u32[]{:S(2)}, u32[]{:S(2)}) collective-permute-start(bf16[384,1152]{1,0:T(8,128)(2,1)} %get-tuple-element.19), channel_id=1, source_target_pairs={{0,1},{1,0},{2,3},{3,2},{4,5},{5,4},{6,7},{7,6},{8,9},{9,8},{10,11... | collective-permute-start | bytes 2654216 | tf_op jit(solution)/shard_map/ppermute | solution.py:49
  49.7 0.1 pad_maximum_fusion.constants
  49.8 0.1 add_convert_fusion.choices
  49.9 1.1 fusion.30
  50.9 0.7 fusion.35
  51.6 0.7 fusion.36
  52.3 11.5 %collective-permute-done.1 = bf16[384,1152]{1,0:T(8,128)(2,1)} collective-permute-done((bf16[384,1152]{1,0:T(8,128)(2,1)S(1)}, bf16[384,1152]{1,0:T(8,128)(2,1)}, u32[]{:S(2)}, u32[]{:S(2)}) %collective-permute-start.1) | collective-permute-done | bytes 884768 | tf_op jit(solution)/shard_map/ppermute | solution.py:49
  63.9 2.1 fusion.21
  66.0 0.0 collective-permute-done.2
  66.0 13.4 %collective-permute-done.3 = bf16[384,1152]{1,0:T(8,128)(2,1)} collective-permute-done((bf16[384,1152]{1,0:T(8,128)(2,1)}, bf16[384,1152]{1,0:T(8,128)(2,1)}, u32[]{:S(2)}, u32[]{:S(2)}) %collective-permute-start.3) | collective-permute-done | bytes 884768 | tf_op jit(solution)/shard_map/ppermute | solution.py:49
  79.4 2.2 fusion.22
  81.6 104.4 %collective-permute-done = bf16[384,1152]{1,0:T(8,128)(2,1)} collective-permute-done((bf16[384,1152]{1,0:T(8,128)(2,1)S(1)}, bf16[384,1152]{1,0:T(8,128)(2,1)}, u32[]{:S(2)}, u32[]{:S(2)}) %collective-permute-start) | collective-permute-done | bytes 884768 | tf_op jit(solution)/shard_map/ppermute | solution.py:165
  186.0 1.4 fusion.10
  187.4 1.3 collective-permute-start.4
  188.7 1.4 fusion.11
  190.1 1.9 collective-permute-start.6
  192.0 1.9 convolution_add_fusion.1
  193.9 2.3 fusion.3
  196.2 0.4 fusion.6.out_b
  196.6 1.3 broadcast_select_fusion.held
  197.9 26.0 %collective-permute-done.6 = bf16[384,1152]{1,0:T(8,128)(2,1)S(1)} collective-permute-done((bf16[384,1152]{1,0:T(8,128)(2,1)}, bf16[384,1152]{1,0:T(8,128)(2,1)S(1)}, u32[]{:S(2)}, u32[]{:S(2)}) %collective-permute-start.6) | collective-permute-done | bytes 884768 | tf_op jit(solution)/shard_map/ppermute | solution.py:193
  223.8 0.3 fusion.12
  224.1 0.0 collective-permute-done.5
  224.1 0.5 fusion.20
  224.6 1.0 fusion.23
  225.6 0.7 convolution_add_fusion.2.grad_a
  226.3 0.0 collective-permute-done.4.relayed
  226.3 0.1 broadcast_in_dim.2.factor_a
  226.4 4.6 %shard_map.67 = (f32[1,384]{1,0:T(1,128)S(1)}, bf16[384,1152]{1,0:T(8,128)(2,1)}, bf16[384,1152]{1,0:T(8,128)(2,1)}) custom-call(s32[2]{0:T(128)S(1)} %add_convert_fusion.choices, f32[2]{0:T(128)S(1)} %pad_maximum_fusion.constants, bf16[384,1152]{1,0:T(8,128)(2,1)S(1)} %collective-permute-done.4.relayed, bf16[384,1152]{1,0:T(8,128)(2,1)S(1)} %broadcast_select_fusion.held, ...), custom_call_target="tpu_custom_call" | custom-call | flops 679477248 | bytes 3538944 | tf_op jit(solution)/shard_map/pallas_call | solution.py:133
  231.1 0.6 reduce
  (7 shorter events, 0.0 us)
Async XLA Ops:
  0.6 33.8 %copy-start = (bf16[384,1152]{1,0:T(8,128)(2,1)S(1)}, bf16[384,1152]{1,0:T(8,128)(2,1)}, u32[]{:S(2)}) copy-start(bf16[384,1152]{1,0:T(8,128)(2,1)} %param.4) | copy-start | bytes 2654212
  0.6 33.8 %copy-start.1 = (bf16[384,1152]{1,0:T(8,128)(2,1)S(1)}, bf16[384,1152]{1,0:T(8,128)(2,1)}, u32[]{:S(2)}) copy-start(bf16[384,1152]{1,0:T(8,128)(2,1)} %param.5) | copy-start | bytes 2654212
  2.1 183.9 %collective-permute-start = (bf16[384,1152]{1,0:T(8,128)(2,1)S(1)}, bf16[384,1152]{1,0:T(8,128)(2,1)}, u32[]{:S(2)}, u32[]{:S(2)}) collective-permute-start(bf16[384,1152]{1,0:T(8,128)(2,1)S(1)} %broadcast_select_fusion.5.raw_a), channel_id=1, source_target_pairs={{2,4},{3,5},{0,62},{1,63},{6,8},{7,9},{4,2},{5,3},{10,12},{11,13},... | collective-permute-start | bytes 2654216 | tf_op jit(solution)/shard_map/ppermute | solution.py:165
  36.5 27.4 %collective-permute-start.1 = (bf16[384,1152]{1,0:T(8,128)(2,1)S(1)}, bf16[384,1152]{1,0:T(8,128)(2,1)}, u32[]{:S(2)}, u32[]{:S(2)}) collective-permute-start(bf16[384,1152]{1,0:T(8,128)(2,1)S(1)} %get-tuple-element.21), channel_id=1, source_target_pairs={{0,2},{1,3},{2,0},{3,1},{4,6},{5,7},{6,4},{7,5},{8,10},{9,11},{10,... | collective-permute-start | bytes 2654216 | tf_op jit(solution)/shard_map/ppermute | solution.py:49
  38.4 185.7 %collective-permute-start.5 = (bf16[384,1152]{1,0:T(8,128)(2,1)S(1)}, bf16[384,1152]{1,0:T(8,128)(2,1)}, u32[]{:S(2)}, u32[]{:S(2)}) collective-permute-start(bf16[384,1152]{1,0:T(8,128)(2,1)S(1)} %get-tuple-element.20.low_a), channel_id=1, source_target_pairs={{0,1022},{1,1023},{1022,0},{1023,1}} | collective-permute-start | bytes 2654216 | tf_op jit(solution)/shard_map/ppermute | solution.py:171
  41.1 24.9 %collective-permute-start.2 = (bf16[384,1152]{1,0:T(8,128)(2,1)}, bf16[384,1152]{1,0:T(8,128)(2,1)}, u32[]{:S(2)}, u32[]{:S(2)}) collective-permute-start(bf16[384,1152]{1,0:T(8,128)(2,1)} %broadcast_select_fusion.3), channel_id=1, source_target_pairs={{0,1023},{1023,0},{1,2},{2,1},{5,6},{6,5},{9,10},{10,9},{13,14},{1... | collective-permute-start | bytes 2654216 | tf_op jit(solution)/shard_map/ppermute | solution.py:172
  42.6 36.8 %collective-permute-start.3 = (bf16[384,1152]{1,0:T(8,128)(2,1)}, bf16[384,1152]{1,0:T(8,128)(2,1)}, u32[]{:S(2)}, u32[]{:S(2)}) collective-permute-start(bf16[384,1152]{1,0:T(8,128)(2,1)} %get-tuple-element.19), channel_id=1, source_target_pairs={{0,1},{1,0},{2,3},{3,2},{4,5},{5,4},{6,7},{7,6},{8,9},{9,8},{10,11... | collective-permute-start | bytes 2654216 | tf_op jit(solution)/shard_map/ppermute | solution.py:49
  187.4 38.9 %collective-permute-start.4 = (bf16[384,1152]{1,0:T(8,128)(2,1)}, bf16[384,1152]{1,0:T(8,128)(2,1)S(1)}, u32[]{:S(2)}, u32[]{:S(2)}) collective-permute-start(bf16[384,1152]{1,0:T(8,128)(2,1)} %collective-permute-done), channel_id=1, source_target_pairs={{5,4},{9,8},{2,3},{13,12},{6,7},{17,16},{10,11},{21,20},{14,15},{2... | collective-permute-start | bytes 2654216 | tf_op jit(solution)/shard_map/ppermute | solution.py:191
  190.1 33.7 %collective-permute-start.6 = (bf16[384,1152]{1,0:T(8,128)(2,1)}, bf16[384,1152]{1,0:T(8,128)(2,1)S(1)}, u32[]{:S(2)}, u32[]{:S(2)}) collective-permute-start(bf16[384,1152]{1,0:T(8,128)(2,1)} %collective-permute-done), channel_id=1, source_target_pairs={{0,64},{1,65},{126,62},{127,63},{64,128},{65,129},{190,126},{191,1... | collective-permute-start | bytes 2654216 | tf_op jit(solution)/shard_map/ppermute | solution.py:193

commit v5 on v3

--- a/solution.py
+++ b/solution.py
@@ -8,7 +8,7 @@
 AXES = ("dp", "group")
 RUN = 4
 LAYER = 16
-ROW_STEP = 128
+ROW_STEP = 384
 LANES = 128
 
 
@@ -104,7 +104,9 @@
                 low_a[at, :], one[...], (((1,), (1,)), ((), ())), preferred_element_type=jnp.float32
             )
             logits = scale_value * dots + bias_value
-            weights = (scale_value * jax.nn.sigmoid(logits)).astype(jnp.bfloat16)
+            decay = jnp.exp(-jnp.abs(logits))
+            chance = jnp.where(logits >= 0.0, 1.0, decay) / (1.0 + decay)
+            weights = (scale_value * chance).astype(jnp.bfloat16)
             part = jnp.dot(weights, one[...], preferred_element_type=jnp.float32)
             factor = factor_a[at, 0:1]
             unit = raw_a[at, :].astype(jnp.float32) * factor
@@ -112,7 +114,7 @@
             b_out[at, :] = out_b[at, :]
             total = before[:, at]
             if is_image:
-                plus = jnp.maximum(logits, 0.0) + jnp.log1p(jnp.exp(-jnp.abs(logits)))
+                plus = jnp.maximum(logits, 0.0) + jnp.log1p(decay)
                 losses = jnp.sum(plus, axis=1, keepdims=True)
                 total = total + jnp.broadcast_to(losses, (ROW_STEP, ROW_STEP)).T[0:1, :]
             loss_out[:, at] = total / (3.0 * rows)

time: 220 us -> 219 us (level)
  no operation moved by 1% of the time
where the time goes in v5:
time: 219 us
  waiting for transfers between devices  147 us (67%)
  starting transfers between devices  40.8 us (19%)
  matrix products  15.3 us (7%)
  other arithmetic  9.19 us (4%)
  Pallas kernels  4.23 us (2%)
    ppermute x1, waiting for transfers between devices, shards(): far = lax.ppermute(raw_a, AXES, far_pairs)  125 us
    ppermute x1, starting transfers between devices, shards(): far = lax.ppermute(raw_a, AXES, far_pairs)  30.5 us
    ppermute x2, waiting for transfers between devices, within(): return lax.ppermute(value, AXES, pairs)  11.9 us
    dot_general x4, matrix products, logits_of(): jnp.einsum('id,jd->ij', rows, columns, preferred_element_type=jnp.float32)  8.19 us
    ppermute x1, waiting for transfers between devices, shards(): relayed = lax.ppermute(far, AXES, relay_pairs)  6.9 us
    dot_general x4, matrix products, apply(): jnp.einsum('ij,jd->id', weights, values, preferred_element_type=jnp.float32)  6.38 us
  transfers between devices with their start and end apart: 7, of which 4 were waited for; matrix products, arithmetic and copies ran while one was open for 10% of the time, Pallas kernels for 0%

profile of v5, /device:TPU:96, one launch (start us, length us, event | category | flops | bytes accessed | tf_op | source)
XLA Modules:
  0.0 218.7 jit_solution(11974558006139406781)
XLA Ops:
  0.6 0.0 copy-start
  0.7 0.0 copy-start.1
  0.7 1.4 broadcast_select_fusion.6.raw_a
  2.1 30.5 %collective-permute-start = (bf16[384,1152]{1,0:T(8,128)(2,1)S(1)}, bf16[384,1152]{1,0:T(8,128)(2,1)S(1)}, u32[]{:S(2)}, u32[]{:S(2)}) collective-permute-start(bf16[384,1152]{1,0:T(8,128)(2,1)S(1)} %broadcast_select_fusion.6.raw_a), channel_id=1, source_target_pairs={{2,4},{3,5},{0,62},{1,63},{6,8},{7,9},{4,2},{5,3},{10,12},{11,13},... | collective-permute-start | bytes 2654216 | tf_op jit(solution)/shard_map/ppermute | solution.py:167
  32.6 0.0 copy-done
  32.6 0.0 copy-done.1
  32.6 0.4 fusion.9
  33.1 0.3 fusion.3
  33.3 1.7 broadcast_select_fusion.3
  35.0 1.9 collective-permute-start.5
  36.9 1.6 collective-permute-start.4
  38.5 2.2 broadcast_select_fusion.4
  40.7 1.9 collective-permute-start.2
  42.6 1.6 collective-permute-start.3
  45.5 0.1 pad_maximum_fusion.constants
  45.6 0.1 add_convert_fusion.choices
  45.7 2.2 %fusion.27 = (f32[384]{0:T(512)S(1)}, f32[384]{0:T(512)S(1)}, f32[384,384]{1,0:T(8,128)S(1)}) fusion(f32[]{:T(128)} %bitcast.23, bf16[384,1152]{1,0:T(8,128)(2,1)S(1)} %get-tuple-element.17.low_a, bf16[384,1152]{1,0:T(8,128)(2,1)} %get-tuple-element.16, f32[]{:T(128)} %bitcast.16), kind=kOutput, calls=%fused_computation.57 | convolution fusion | flops 341949696 | bytes 2362376 | tf_op jit(solution)/shard_map/id,jd->ij/dot_general | solution.py:68
  47.9 0.7 fusion.32
  48.6 1.8 fusion.33
  50.5 11.9 %collective-permute-done.5 = bf16[384,1152]{1,0:T(8,128)(2,1)} collective-permute-done((bf16[384,1152]{1,0:T(8,128)(2,1)}, bf16[384,1152]{1,0:T(8,128)(2,1)}, u32[]{:S(2)}, u32[]{:S(2)}) %collective-permute-start.5) | collective-permute-done | bytes 884768 | tf_op jit(solution)/shard_map/ppermute | solution.py:49
  62.3 2.4 %fusion.18 = (f32[384]{0:T(512)S(1)}, f32[384,384]{1,0:T(8,128)S(1)}) fusion(f32[]{:T(128)} %bitcast.26, bf16[384,1152]{1,0:T(8,128)(2,1)} %get-tuple-element.16, bf16[384,1152]{1,0:T(8,128)(2,1)} %collective-permute-done.5, f32[]{:T(128)} %bitcast.22), kind=kOutput, calls=%fused_computation.42 | convolution fusion | flops 341065344 | bytes 2360840 | tf_op jit(solution)/shard_map/id,jd->ij/dot_general | solution.py:68
  64.8 124.7 %collective-permute-done = bf16[384,1152]{1,0:T(8,128)(2,1)S(1)} collective-permute-done((bf16[384,1152]{1,0:T(8,128)(2,1)S(1)}, bf16[384,1152]{1,0:T(8,128)(2,1)S(1)}, u32[]{:S(2)}, u32[]{:S(2)}) %collective-permute-start) | collective-permute-done | bytes 884768 | tf_op jit(solution)/shard_map/ppermute | solution.py:167
  189.4 1.9 collective-permute-start.6
  191.4 1.3 collective-permute-start.1
  192.7 1.8 convolution_add_fusion.1
  194.5 0.0 collective-permute-done.2
  194.5 0.0 collective-permute-done.3
  194.5 2.5 %fusion.20 = (f32[384]{0:T(512)S(1)}, f32[384,384]{1,0:T(8,128)S(1)}) fusion(f32[]{:T(128)} %bitcast.24, bf16[384,1152]{1,0:T(8,128)(2,1)} %get-tuple-element.16, bf16[384,1152]{1,0:T(8,128)(2,1)} %collective-permute-done.3, bf16[384,1152]{1,0:T(8,128)(2,1)} %collective-permute-done.2, pred[]{:T(512)S(6)} %or.9, f32[]{:T(128)} %bitcast.18), kind=kOutput, calls=%fused_computation.44 | convolution fusion | flops 341507712 | bytes 3245577 | tf_op jit(solution)/shard_map/id,jd->ij/dot_general | solution.py:68
  197.0 2.1 fusion.5
  199.0 0.4 fusion.8.out_b
  199.5 1.3 broadcast_select_fusion.2.held
  200.7 3.6 %collective-permute-done.6 = bf16[384,1152]{1,0:T(8,128)(2,1)S(1)} collective-permute-done((bf16[384,1152]{1,0:T(8,128)(2,1)S(1)}, bf16[384,1152]{1,0:T(8,128)(2,1)S(1)}, u32[]{:S(2)}, u32[]{:S(2)}) %collective-permute-start.6) | collective-permute-done | bytes 884768 | tf_op jit(solution)/shard_map/ppermute | solution.py:189
  204.4 0.4 fusion.10
  204.8 0.0 collective-permute-done.4
  204.8 0.4 fusion.17
  205.2 1.0 fusion.19
  206.2 0.7 convolution_add_fusion.2.grad_a
  206.9 6.9 %collective-permute-done.1.relayed = bf16[384,1152]{1,0:T(8,128)(2,1)S(1)} collective-permute-done((bf16[384,1152]{1,0:T(8,128)(2,1)S(1)}, bf16[384,1152]{1,0:T(8,128)(2,1)S(1)}, u32[]{:S(2)}, u32[]{:S(2)}) %collective-permute-start.1) | collective-permute-done | bytes 884768 | tf_op jit(solution)/shard_map/ppermute | solution.py:184
  213.8 0.1 broadcast_in_dim.2.factor_a
  213.9 4.2 %shard_map.67 = (f32[1,384]{1,0:T(1,128)S(1)}, bf16[384,1152]{1,0:T(8,128)(2,1)}, bf16[384,1152]{1,0:T(8,128)(2,1)}) custom-call(s32[2]{0:T(128)S(1)} %add_convert_fusion.choices, f32[2]{0:T(128)S(1)} %pad_maximum_fusion.constants, bf16[384,1152]{1,0:T(8,128)(2,1)S(1)} %collective-permute-done.1.relayed, bf16[384,1152]{1,0:T(8,128)(2,1)S(1)} %broadcast_select_fusion.2.held, ...), custom_call_target="tpu_custom_call" | custom-call | flops 679477248 | bytes 3538944 | tf_op jit(solution)/shard_map/pallas_call | solution.py:135
  218.1 0.6 reduce
  (4 shorter events, 0.0 us)
Async XLA Ops:
  0.6 32.0 %copy-start = (bf16[384,1152]{1,0:T(8,128)(2,1)S(1)}, bf16[384,1152]{1,0:T(8,128)(2,1)}, u32[]{:S(2)}) copy-start(bf16[384,1152]{1,0:T(8,128)(2,1)} %param.4) | copy-start | bytes 2654212
  0.7 32.0 %copy-start.1 = (bf16[384,1152]{1,0:T(8,128)(2,1)S(1)}, bf16[384,1152]{1,0:T(8,128)(2,1)}, u32[]{:S(2)}) copy-start(bf16[384,1152]{1,0:T(8,128)(2,1)} %param.5) | copy-start | bytes 2654212
  2.1 187.4 %collective-permute-start = (bf16[384,1152]{1,0:T(8,128)(2,1)S(1)}, bf16[384,1152]{1,0:T(8,128)(2,1)S(1)}, u32[]{:S(2)}, u32[]{:S(2)}) collective-permute-start(bf16[384,1152]{1,0:T(8,128)(2,1)S(1)} %broadcast_select_fusion.6.raw_a), channel_id=1, source_target_pairs={{2,4},{3,5},{0,62},{1,63},{6,8},{7,9},{4,2},{5,3},{10,12},{11,13},... | collective-permute-start | bytes 2654216 | tf_op jit(solution)/shard_map/ppermute | solution.py:167
  35.0 27.3 %collective-permute-start.5 = (bf16[384,1152]{1,0:T(8,128)(2,1)}, bf16[384,1152]{1,0:T(8,128)(2,1)}, u32[]{:S(2)}, u32[]{:S(2)}) collective-permute-start(bf16[384,1152]{1,0:T(8,128)(2,1)} %get-tuple-element.16), channel_id=1, source_target_pairs={{0,2},{1,3},{2,0},{3,1},{4,6},{5,7},{6,4},{7,5},{8,10},{9,11},{10,... | collective-permute-start | bytes 2654216 | tf_op jit(solution)/shard_map/ppermute | solution.py:49
  36.9 167.8 %collective-permute-start.4 = (bf16[384,1152]{1,0:T(8,128)(2,1)S(1)}, bf16[384,1152]{1,0:T(8,128)(2,1)}, u32[]{:S(2)}, u32[]{:S(2)}) collective-permute-start(bf16[384,1152]{1,0:T(8,128)(2,1)S(1)} %get-tuple-element.17.low_a), channel_id=1, source_target_pairs={{0,1022},{1,1023},{1022,0},{1023,1}} | collective-permute-start | bytes 2654216 | tf_op jit(solution)/shard_map/ppermute | solution.py:173
  40.7 153.8 %collective-permute-start.2 = (bf16[384,1152]{1,0:T(8,128)(2,1)}, bf16[384,1152]{1,0:T(8,128)(2,1)}, u32[]{:S(2)}, u32[]{:S(2)}) collective-permute-start(bf16[384,1152]{1,0:T(8,128)(2,1)} %broadcast_select_fusion.4), channel_id=1, source_target_pairs={{0,1},{1,0},{2,3},{3,2},{4,5},{5,4},{6,7},{7,6},{8,9},{9,8},{10,11... | collective-permute-start | bytes 2654216 | tf_op jit(solution)/shard_map/ppermute | solution.py:49
  42.6 151.9 %collective-permute-start.3 = (bf16[384,1152]{1,0:T(8,128)(2,1)}, bf16[384,1152]{1,0:T(8,128)(2,1)}, u32[]{:S(2)}, u32[]{:S(2)}) collective-permute-start(bf16[384,1152]{1,0:T(8,128)(2,1)} %get-tuple-element.15), channel_id=1, source_target_pairs={{0,1023},{1023,0},{1,2},{2,1},{5,6},{6,5},{9,10},{10,9},{13,14},{1... | collective-permute-start | bytes 2654216 | tf_op jit(solution)/shard_map/ppermute | solution.py:174
  189.4 14.9 %collective-permute-start.6 = (bf16[384,1152]{1,0:T(8,128)(2,1)S(1)}, bf16[384,1152]{1,0:T(8,128)(2,1)S(1)}, u32[]{:S(2)}, u32[]{:S(2)}) collective-permute-start(bf16[384,1152]{1,0:T(8,128)(2,1)S(1)} %collective-permute-done), channel_id=1, source_target_pairs={{0,64},{1,65},{126,62},{127,63},{64,128},{65,129},{190,126},{191,1... | collective-permute-start | bytes 2654216 | tf_op jit(solution)/shard_map/ppermute | solution.py:189
  191.4 22.5 %collective-permute-start.1 = (bf16[384,1152]{1,0:T(8,128)(2,1)S(1)}, bf16[384,1152]{1,0:T(8,128)(2,1)S(1)}, u32[]{:S(2)}, u32[]{:S(2)}) collective-permute-start(bf16[384,1152]{1,0:T(8,128)(2,1)S(1)} %collective-permute-done), channel_id=1, source_target_pairs={{5,4},{9,8},{2,3},{13,12},{6,7},{17,16},{10,11},{21,20},{14,15},{2... | collective-permute-start | bytes 2654216 | tf_op jit(solution)/shard_map/ppermute | solution.py:184

commit v6 on v4

--- a/solution.py
+++ b/solution.py
@@ -9,6 +9,7 @@
 RUN = 4
 LAYER = 16
 ROW_STEP = 128
+SPLIT = 256
 LANES = 128
 
 
@@ -93,7 +94,7 @@
 
     @pl.when(jnp.logical_not(use_held))
     def _():
-        for start in range(0, rows, ROW_STEP):
+        for start in range(0, one.shape[0], ROW_STEP):
             at = pl.ds(start, ROW_STEP)
             one[at, :] = low(relayed[at, :])
 
@@ -139,10 +140,12 @@
         ),
         in_specs=[smem] * 2 + [vmem] * 8,
         out_specs=(vmem,) * 3,
-        scratch_shapes=[pltpu.VMEM((rows, features), jnp.bfloat16)],
+        scratch_shapes=[pltpu.VMEM(relayed.shape, jnp.bfloat16)],
         compiler_params=pltpu.CompilerParams(vmem_limit_bytes=24 * 1024 * 1024),
         cost_estimate=pl.CostEstimate(
-            flops=4 * rows * rows * features, bytes_accessed=8 * rows * features, transcendentals=3 * rows * rows
+            flops=4 * rows * held.shape[0] * features,
+            bytes_accessed=8 * rows * features,
+            transcendentals=3 * rows * held.shape[0],
         ),
     )(choices, constants, relayed, held, low_a, raw_a, factor_a, grad_a, out_b, before.reshape(1, rows))
     return (loss.reshape(rows), image_grad, text_grad)
@@ -179,6 +182,9 @@
     grad_a = apply(weights, low_b)
     grad_b = jnp.einsum("ij,id->jd", weights, low_a, preferred_element_type=jnp.float32)
 
+    relayed = [lax.ppermute(rows, AXES, relay_pairs) for rows in (far[:SPLIT], far[SPLIT:])]
+    shift_from, low_far = lax.optimization_barrier((far, low(far)))
+    moved = lax.ppermute(shift_from, AXES, shift_pairs)
 
     loss_two, part = negative_pairs(low_b, near_two, scale_value, bias_value)
     grad_b = grad_b + part
@@ -187,20 +193,21 @@
     grad_b = grad_b + part
     out_b = unit_backward(grad_b, unit_b, factor_b)
     loss_b = loss_two + loss_one
-    far, loss_b = lax.optimization_barrier((far, loss_b))
-    relayed = lax.ppermute(far, AXES, relay_pairs)
-    shift_from, low_far = lax.optimization_barrier((far, low(far)))
-    moved = lax.ppermute(shift_from, AXES, shift_pairs)
 
     held = jnp.where(inner, near_one, middle)
     two = jnp.where(wrapped, wrap, jnp.where(shifted, low(moved), low_far))
     loss_a, part = negative_pairs(low_a, two, scale_value, bias_value)
     grad_a = grad_a + part
+    use_held = inner | end
+    one = jnp.where(use_held, held[:SPLIT], low(relayed[0]))
+    loss, part = negative_pairs(low_a, one, scale_value, bias_value)
+    grad_a, loss_a = grad_a + part, loss_a + loss
     before = own_loss + jnp.where(first_half, loss_a, loss_b)
-    choices = jnp.stack([inner | end, first_half]).astype(jnp.int32)
+    choices = jnp.stack([use_held, first_half]).astype(jnp.int32)
     constants = jnp.stack([scale_value, bias_value])
     factor_wide = jnp.broadcast_to(factor_a, (count_rows, LANES))
-    return finish(choices, constants, relayed, held, low_a, raw_a, factor_wide, grad_a, out_b, before)
+    last, grad_a, before, factor_wide = lax.optimization_barrier((relayed[1], grad_a, before, factor_wide))
+    return finish(choices, constants, last, held[SPLIT:], low_a, raw_a, factor_wide, grad_a, out_b, before)
 
 
 def solution(mesh):

time: 232 us -> 220 us (0.948)
  the two profiles are of different devices: /device:TPU:32 before, /device:TPU:96 now
where the time goes in v6:
time: 220 us; the launch traced here: 219 us
  waiting for transfers between devices  144 us (65%)
  starting transfers between devices  42.2 us (19%)
  matrix products  16.6 us (8%)
  other arithmetic  9.79 us (4%)
  Pallas kernels  3.56 us (2%)
  between operations  2.21 us (1%)
    ppermute x1, waiting for transfers between devices, shards(): far = lax.ppermute(raw_a, AXES, far_pairs)  139 us
    ppermute x1, starting transfers between devices, shards(): far = lax.ppermute(raw_a, AXES, far_pairs)  30.5 us
    dot_general x5, matrix products, logits_of(): jnp.einsum('id,jd->ij', rows, columns, preferred_element_type=jnp.float32)  8.94 us
    dot_general x5, matrix products, apply(): jnp.einsum('ij,jd->id', weights, values, preferred_element_type=jnp.float32)  6.94 us
    ppermute x2, waiting for transfers between devices, shards(): lax.ppermute(rows, AXES, relay_pairs)  5.55 us
  transfers between devices with their start and end apart: 8, of which 2 were waited for; matrix products, arithmetic and copies ran while one was open for 11% of the time, Pallas kernels for 0%

profile of v6, /device:TPU:96, one launch (start us, length us, event | category | flops | bytes accessed | tf_op | source)
XLA Modules:
  0.0 219.1 jit_solution(18225749095604514408)
XLA Ops:
  0.6 0.0 copy-start
  0.7 0.0 copy-start.1
  0.7 1.4 broadcast_select_fusion.5.raw_a
  2.1 30.5 %collective-permute-start = (bf16[384,1152]{1,0:T(8,128)(2,1)S(1)}, bf16[384,1152]{1,0:T(8,128)(2,1)S(1)}, u32[]{:S(2)}, u32[]{:S(2)}) collective-permute-start(bf16[384,1152]{1,0:T(8,128)(2,1)S(1)} %broadcast_select_fusion.5.raw_a), channel_id=1, source_target_pairs={{2,4},{3,5},{0,62},{1,63},{6,8},{7,9},{4,2},{5,3},{10,12},{11,13},... | collective-permute-start | bytes 2654216 | tf_op jit(solution)/shard_map/ppermute | solution.py:168
  32.6 0.0 copy-done
  32.6 0.0 copy-done.1
  32.6 0.4 fusion.9
  33.1 0.3 fusion.3
  33.3 1.7 broadcast_select_fusion.2
  35.0 1.9 collective-permute-start.7
  36.9 1.6 collective-permute-start.2
  38.5 2.2 broadcast_select_fusion.3
  40.7 1.9 collective-permute-start.4
  42.6 1.6 collective-permute-start.5
  45.5 0.1 pad_maximum_fusion.constants
  45.6 0.1 add_convert_fusion.choices
  45.7 2.2 %fusion.35 = (f32[384]{0:T(512)S(1)}, f32[384]{0:T(512)S(1)}, f32[384,384]{1,0:T(8,128)S(1)}) fusion(f32[]{:T(128)} %bitcast.26, bf16[384,1152]{1,0:T(8,128)(2,1)S(1)} %get-tuple-element.24.low_a, bf16[384,1152]{1,0:T(8,128)(2,1)} %get-tuple-element.25, f32[]{:T(128)} %bitcast.17), kind=kOutput, calls=%fused_computation.72 | convolution fusion | flops 341949696 | bytes 2362376 | tf_op jit(solution)/shard_map/id,jd->ij/dot_general | solution.py:69
  47.9 0.7 fusion.45
  48.6 1.8 fusion.46
  50.5 138.9 %collective-permute-done = bf16[384,1152]{1,0:T(8,128)(2,1)S(1)} collective-permute-done((bf16[384,1152]{1,0:T(8,128)(2,1)S(1)}, bf16[384,1152]{1,0:T(8,128)(2,1)S(1)}, u32[]{:S(2)}, u32[]{:S(2)}) %collective-permute-start) | collective-permute-done | bytes 884768 | tf_op jit(solution)/shard_map/ppermute | solution.py:168
  189.4 1.3 collective-permute-start.6
  190.7 0.3 fusion.10
  191.0 0.2 fusion.11
  191.3 0.0 collective-permute-done.7
  191.3 1.9 collective-permute-start.3
  193.2 2.5 %fusion.26 = (f32[384]{0:T(512)S(1)}, f32[384,384]{1,0:T(8,128)S(1)}) fusion(f32[]{:T(128)} %bitcast.29, bf16[384,1152]{1,0:T(8,128)(2,1)} %get-tuple-element.25, bf16[384,1152]{1,0:T(8,128)(2,1)} %collective-permute-done.7, f32[]{:T(128)} %bitcast.22), kind=kOutput, calls=%fused_computation.56 | convolution fusion | flops 341065344 | bytes 2360840 | tf_op jit(solution)/shard_map/id,jd->ij/dot_general | solution.py:69
  195.7 1.8 convolution_add_fusion.2
  197.5 0.0 collective-permute-done.4
  197.5 1.5 collective-permute-start.1
  199.0 0.0 collective-permute-done.5
  199.0 2.5 %fusion.27 = (f32[384]{0:T(512)S(1)}, f32[384,384]{1,0:T(8,128)S(1)}) fusion(f32[]{:T(128)} %bitcast.28, bf16[384,1152]{1,0:T(8,128)(2,1)} %get-tuple-element.25, bf16[384,1152]{1,0:T(8,128)(2,1)} %collective-permute-done.5, bf16[384,1152]{1,0:T(8,128)(2,1)} %collective-permute-done.4, pred[]{:T(512)S(6)} %or.9, f32[]{:T(128)} %bitcast.21), kind=kOutput, calls=%fused_computation.57 | convolution fusion | flops 341507712 | bytes 3245577 | tf_op jit(solution)/shard_map/id,jd->ij/dot_general | solution.py:69
  201.5 2.1 fusion.5
  203.5 0.4 fusion.8.out_b
  203.9 1.3 broadcast_select_fusion.1
  205.3 0.0 collective-permute-done.6
  205.3 0.2 fusion.20
  205.5 0.8 fusion.28
  206.2 0.0 collective-permute-done.3
  206.2 0.3 fusion.12
  206.5 0.0 collective-permute-done.2
  206.5 0.5 fusion.23
  207.0 1.0 fusion.25
  208.0 0.7 convolution_add_fusion.3
  208.7 0.6 convolution_add_fusion.grad_a
  209.3 5.5 %collective-permute-done.1.relayed = bf16[128,1152]{1,0:T(8,128)(2,1)S(1)} collective-permute-done((bf16[128,1152]{1,0:T(8,128)(2,1)S(1)}, bf16[128,1152]{1,0:T(8,128)(2,1)S(1)}, u32[]{:S(2)}, u32[]{:S(2)}) %collective-permute-start.1) | collective-permute-done | bytes 294944 | tf_op jit(solution)/shard_map/ppermute | solution.py:185
  214.8 0.1 broadcast_in_dim.2.factor_a
  214.9 3.6 %shard_map.67 = (f32[1,384]{1,0:T(1,128)S(1)}, bf16[384,1152]{1,0:T(8,128)(2,1)}, bf16[384,1152]{1,0:T(8,128)(2,1)}) custom-call(s32[2]{0:T(128)S(1)} %add_convert_fusion.choices, f32[2]{0:T(128)S(1)} %pad_maximum_fusion.constants, bf16[128,1152]{1,0:T(8,128)(2,1)S(1)} %collective-permute-done.1.relayed, bf16[128,1152]{1,0:T(8,128)(2,1)S(1)} %slice.19.held, ...), custom_call_target="tpu_custom_call" | custom-call | flops 226492416 | bytes 3538944 | tf_op jit(solution)/shard_map/pallas_call | solution.py:134
  218.5 0.6 reduce
  (10 shorter events, 0.1 us)
Async XLA Ops:
  0.6 32.0 %copy-start = (bf16[384,1152]{1,0:T(8,128)(2,1)S(1)}, bf16[384,1152]{1,0:T(8,128)(2,1)}, u32[]{:S(2)}) copy-start(bf16[384,1152]{1,0:T(8,128)(2,1)} %param.4) | copy-start | bytes 2654212
  0.7 32.0 %copy-start.1 = (bf16[384,1152]{1,0:T(8,128)(2,1)S(1)}, bf16[384,1152]{1,0:T(8,128)(2,1)}, u32[]{:S(2)}) copy-start(bf16[384,1152]{1,0:T(8,128)(2,1)} %param.5) | copy-start | bytes 2654212
  2.1 187.3 %collective-permute-start = (bf16[384,1152]{1,0:T(8,128)(2,1)S(1)}, bf16[384,1152]{1,0:T(8,128)(2,1)S(1)}, u32[]{:S(2)}, u32[]{:S(2)}) collective-permute-start(bf16[384,1152]{1,0:T(8,128)(2,1)S(1)} %broadcast_select_fusion.5.raw_a), channel_id=1, source_target_pairs={{2,4},{3,5},{0,62},{1,63},{6,8},{7,9},{4,2},{5,3},{10,12},{11,13},... | collective-permute-start | bytes 2654216 | tf_op jit(solution)/shard_map/ppermute | solution.py:168
  35.0 156.3 %collective-permute-start.7 = (bf16[384,1152]{1,0:T(8,128)(2,1)}, bf16[384,1152]{1,0:T(8,128)(2,1)}, u32[]{:S(2)}, u32[]{:S(2)}) collective-permute-start(bf16[384,1152]{1,0:T(8,128)(2,1)} %get-tuple-element.25), channel_id=1, source_target_pairs={{0,2},{1,3},{2,0},{3,1},{4,6},{5,7},{6,4},{7,5},{8,10},{9,11},{10,... | collective-permute-start | bytes 2654216 | tf_op jit(solution)/shard_map/ppermute | solution.py:50
  36.9 169.6 %collective-permute-start.2 = (bf16[384,1152]{1,0:T(8,128)(2,1)S(1)}, bf16[384,1152]{1,0:T(8,128)(2,1)}, u32[]{:S(2)}, u32[]{:S(2)}) collective-permute-start(bf16[384,1152]{1,0:T(8,128)(2,1)S(1)} %get-tuple-element.24.low_a), channel_id=1, source_target_pairs={{0,1022},{1,1023},{1022,0},{1023,1}} | collective-permute-start | bytes 2654216 | tf_op jit(solution)/shard_map/ppermute | solution.py:174
  40.7 156.8 %collective-permute-start.4 = (bf16[384,1152]{1,0:T(8,128)(2,1)}, bf16[384,1152]{1,0:T(8,128)(2,1)}, u32[]{:S(2)}, u32[]{:S(2)}) collective-permute-start(bf16[384,1152]{1,0:T(8,128)(2,1)} %broadcast_select_fusion.3), channel_id=1, source_target_pairs={{0,1},{1,0},{2,3},{3,2},{4,5},{5,4},{6,7},{7,6},{8,9},{9,8},{10,11... | collective-permute-start | bytes 2654216 | tf_op jit(solution)/shard_map/ppermute | solution.py:50
  42.6 156.4 %collective-permute-start.5 = (bf16[384,1152]{1,0:T(8,128)(2,1)}, bf16[384,1152]{1,0:T(8,128)(2,1)}, u32[]{:S(2)}, u32[]{:S(2)}) collective-permute-start(bf16[384,1152]{1,0:T(8,128)(2,1)} %get-tuple-element.23), channel_id=1, source_target_pairs={{0,1023},{1023,0},{1,2},{2,1},{5,6},{6,5},{9,10},{10,9},{13,14},{1... | collective-permute-start | bytes 2654216 | tf_op jit(solution)/shard_map/ppermute | solution.py:175
  189.4 15.8 %collective-permute-start.6 = (bf16[256,1152]{1,0:T(8,128)(2,1)S(1)}, bf16[256,1152]{1,0:T(8,128)(2,1)S(1)}, u32[]{:S(2)}, u32[]{:S(2)}) collective-permute-start(bf16[256,1152]{1,0:T(8,128)(2,1)S(1)} %slice.18), channel_id=1, source_target_pairs={{5,4},{9,8},{2,3},{13,12},{6,7},{17,16},{10,11},{21,20},{14,15},{2... | collective-permute-start | bytes 1769480 | tf_op jit(solution)/shard_map/ppermute | solution.py:185
  191.3 15.0 %collective-permute-start.3 = (bf16[384,1152]{1,0:T(8,128)(2,1)S(1)}, bf16[384,1152]{1,0:T(8,128)(2,1)S(1)}, u32[]{:S(2)}, u32[]{:S(2)}) collective-permute-start(bf16[384,1152]{1,0:T(8,128)(2,1)S(1)} %collective-permute-done), channel_id=1, source_target_pairs={{0,64},{1,65},{126,62},{127,63},{64,128},{65,129},{190,126},{191,1... | collective-permute-start | bytes 2654216 | tf_op jit(solution)/shard_map/ppermute | solution.py:187
  197.5 17.3 %collective-permute-start.1 = (bf16[128,1152]{1,0:T(8,128)(2,1)S(1)}, bf16[128,1152]{1,0:T(8,128)(2,1)S(1)}, u32[]{:S(2)}, u32[]{:S(2)}) collective-permute-start(bf16[128,1152]{1,0:T(8,128)(2,1)S(1)} %slice.16), channel_id=1, source_target_pairs={{5,4},{9,8},{2,3},{13,12},{6,7},{17,16},{10,11},{21,20},{14,15},{2... | collective-permute-start | bytes 884744 | tf_op jit(solution)/shard_map/ppermute | solution.py:185
